TPU v7x, 128 devices: a whole 4x4x4 slice. The times are simulated.
128 devices in a mesh: dp: 8 (over x, y_hi), fsdp: 16 (over y_lo, z, core).
Axes of the slice: x: 4, y: 4 (y_hi: 2, y_lo: 2; y = y_hi * 2 + y_lo), z: 4, core: 2. Of those that a mesh axis runs over, the one named last changes fastest.
Arguments:
- qkv_rows: bfloat16 [8, 16, 8, 64, 4992], P('dp', 'fsdp'), may hold values from -6 to 6
- proj_weight: bfloat16 [3200, 1664], P('fsdp'), may hold values from -0.15625 to 0.15625
- layer_scale: float32 [3200], replicated, may hold values from 0.3 to 3
- out_grad: bfloat16 [8, 16, 320, 3200], P('dp', 'fsdp'), may hold values from -6 to 6
- patch_counts: int32 [8, 16, 8], replicated, may hold values from 16 to 64, as said below
- loader_plan: int32 [8, 16, 8], replicated, may hold values from 0 to 7, as said below
- row_offsets: int32 [8, 16, 8], replicated, may hold values from 0 to 304, as said below
Outputs:
- attn_branch: bfloat16 [8, 16, 320, 3200], P('dp', 'fsdp')
- qkv_grad: bfloat16 [8, 16, 8, 64, 4992], P('dp', 'fsdp')
- weight_grad: float32 [3200, 1664], P('fsdp')
Inputs may be any that keep to these rules, and one draw needn't show every extreme that they name: `patch_counts`: the 8 images of each owner pair up so that the two counts of a pair sum to 80; in some owner an image has 64 patches. For each column f and image k, (loader_plan[e, f, k] - e) mod 8 is the same for every owner e and differs between images, so each loader holds one image of every owner in its column. The images of one owner occupy the disjoint row ranges from row_offsets to row_offsets + patch_counts - 1 and together fill all 320 rows.
All inputs are finite; a program needn't handle non-finite values.
Results may differ from a plain program's by a relative error of at most 0.015.
Values may be sent and summed in bfloat16 or wider, within the bound.
A program may use at most 192 MiB of HBM per device.

v0:
```python
import math

import jax
import jax.numpy as jnp
from jax import lax
from jax.sharding import PartitionSpec as P

HEADS = 13
HEAD = 128


MASKED = -1e30


def split_heads(block):
    feature = block.shape[-1] // 3
    shape_lead = block.shape[:-1]
    queries = block[..., :feature].reshape(shape_lead + (HEADS, HEAD))
    key_rows = block[..., feature : 2 * feature].reshape(shape_lead + (HEADS, HEAD))
    value_rows = block[..., 2 * feature :].reshape(shape_lead + (HEADS, HEAD))
    return (queries, key_rows, value_rows)


def attend(block, groups):
    queries, key_rows, value_rows = split_heads(block)
    inv_scale = 1.0 / math.sqrt(HEAD)
    scores = (
        jnp.einsum("bqhd,bkhd->bhqk", queries, key_rows, preferred_element_type=jnp.float32)
        * inv_scale
    )
    allowed = (groups[:, :, None] == groups[:, None, :]) & (groups[:, None, :] >= 0)
    scores = jnp.where(allowed[:, None], scores, MASKED)
    row_max = jnp.max(scores, axis=-1, keepdims=True)
    expo_rows = jnp.exp(scores - row_max)
    soft = expo_rows / jnp.sum(expo_rows, axis=-1, keepdims=True)
    soft_low = soft.astype(jnp.bfloat16)
    mixed_heads = jnp.einsum(
        "bhqk,bkhd->bqhd", soft_low, value_rows, preferred_element_type=jnp.float32
    )
    live_rows = (groups >= 0)[:, :, None, None]
    attn_out = jnp.where(live_rows, mixed_heads, 0.0).astype(jnp.bfloat16)
    attn_out = attn_out.reshape(block.shape[:-1] + (HEADS * HEAD,))
    return (attn_out, soft, soft_low)


def attend_back(block, soft, soft_low, attn_out, grad_out):
    queries, key_rows, value_rows = split_heads(block)
    inv_scale = 1.0 / math.sqrt(HEAD)
    shape_lead = block.shape[:-1]
    grad_heads = grad_out.reshape(shape_lead + (HEADS, HEAD))
    out_heads = attn_out.reshape(shape_lead + (HEADS, HEAD))
    grad_value = jnp.einsum(
        "bhqk,bqhd->bkhd", soft_low, grad_heads, preferred_element_type=jnp.float32
    ).astype(jnp.bfloat16)
    grad_soft = jnp.einsum(
        "bqhd,bkhd->bhqk", grad_heads, value_rows, preferred_element_type=jnp.float32
    )
    delta = jnp.sum(grad_heads.astype(jnp.float32) * out_heads.astype(jnp.float32), axis=-1)
    grad_score = soft * (grad_soft - jnp.transpose(delta, (0, 2, 1))[..., None])
    score_low = grad_score.astype(jnp.bfloat16)
    grad_query = (
        jnp.einsum("bhqk,bkhd->bqhd", score_low, key_rows, preferred_element_type=jnp.float32)
        * inv_scale
    ).astype(jnp.bfloat16)
    grad_key = (
        jnp.einsum("bhqk,bqhd->bkhd", score_low, queries, preferred_element_type=jnp.float32)
        * inv_scale
    ).astype(jnp.bfloat16)
    width_all = HEADS * HEAD
    return jnp.concatenate(
        [
            grad_query.reshape(shape_lead + (width_all,)),
            grad_key.reshape(shape_lead + (width_all,)),
            grad_value.reshape(shape_lead + (width_all,)),
        ],
        axis=-1,
    )


def project(attended, weights, layer_scale):
    projected = lax.dot_general(
        attended, weights, (((1,), (1,)), ((), ())), preferred_element_type=jnp.float32
    )
    return (layer_scale * projected).astype(jnp.bfloat16)


def per_device(
    qkv_rows, proj_weight, layer_scale, out_grad, patch_counts, loader_plan, row_offsets
):
    dp_count = lax.axis_size("dp")
    dp_index = lax.axis_index("dp")
    column = lax.axis_index("fsdp")
    col_plan = lax.dynamic_index_in_dim(loader_plan, column, 1, keepdims=False)
    col_counts = lax.dynamic_index_in_dim(patch_counts, column, 1, keepdims=False)
    col_offsets = lax.dynamic_index_in_dim(row_offsets, column, 1, keepdims=False)
    my_plan = lax.dynamic_index_in_dim(col_plan, dp_index, 0, keepdims=False)
    my_counts = lax.dynamic_index_in_dim(col_counts, dp_index, 0, keepdims=False)
    my_offsets = lax.dynamic_index_in_dim(col_offsets, dp_index, 0, keepdims=False)
    slot_data = qkv_rows[0, 0]
    grad_rows = out_grad[0, 0]
    images_count = slot_data.shape[0]
    slot_len = slot_data.shape[1]
    own_rows = grad_rows.shape[0]
    slot_pos = jnp.arange(slot_len, dtype=jnp.int32)
    image_ids = jnp.arange(images_count, dtype=jnp.int32)
    owner_ids = jnp.arange(dp_count, dtype=jnp.int32)
    row_ids = jnp.arange(own_rows, dtype=jnp.int32)
    matches = (col_plan == dp_index).astype(jnp.int32)
    send_slot = jnp.sum(matches * image_ids[None, :], axis=1)
    owner_of_slot = jnp.sum(matches * owner_ids[:, None], axis=0)
    image_of_source = jnp.sum(
        (my_plan[None, :] == owner_ids[:, None]).astype(jnp.int32) * image_ids[None, :], axis=1
    )
    inside = (
        (row_ids[:, None] >= my_offsets[None, :])
        & (row_ids[:, None] < (my_offsets + my_counts)[None, :])
    ).astype(jnp.int32)
    segment = jnp.sum(inside * image_ids[None, :], axis=1)
    row_base = jnp.sum(inside * my_offsets[None, :], axis=1)
    flat_index = segment * slot_len + row_ids - row_base
    back_index = jnp.clip(my_offsets[:, None] + slot_pos[None, :], 0, own_rows - 1)
    slot_valid = slot_pos[None, :] < my_counts[:, None]
    weights = lax.all_gather(proj_weight, "fsdp", axis=0, tiled=True)
    outgoing = jnp.take(slot_data, send_slot, axis=0)
    incoming = lax.all_to_all(outgoing, "dp", split_axis=0, concat_axis=0, tiled=True)
    images = jnp.take(incoming, my_plan, axis=0)
    block = images.reshape(images_count * slot_len, -1)[flat_index][None]
    attn_out, soft, soft_low = attend(block, segment[None])
    attended = attn_out[0]
    branch_rows = project(attended, weights, layer_scale)
    scaled = (grad_rows.astype(jnp.float32) * layer_scale).astype(jnp.bfloat16)
    grad_attended = jnp.dot(scaled, weights, preferred_element_type=jnp.float32).astype(
        jnp.bfloat16
    )
    grad_block = attend_back(block, soft, soft_low, attn_out, grad_attended[None])[0]
    grad_slots = jnp.where(
        slot_valid[..., None], grad_block[back_index], jnp.zeros((), jnp.bfloat16)
    )
    back_send = jnp.take(grad_slots, image_of_source, axis=0)
    returned = lax.all_to_all(back_send, "dp", split_axis=0, concat_axis=0, tiled=True)
    grad_patches = jnp.take(returned, owner_of_slot, axis=0)
    shard_sum = lax.psum_scatter(
        lax.dot_general(
            scaled, attended, (((0,), (0,)), ((), ())), preferred_element_type=jnp.float32
        ),
        "fsdp",
        scatter_dimension=0,
        tiled=True,
    )
    weight_grad = lax.psum(shard_sum, "dp")
    return (branch_rows[None, None], grad_patches[None, None], weight_grad)


def solution(mesh):
    in_specs = (
        P("dp", "fsdp", None, None, None),
        P("fsdp", None),
        P(),
        P("dp", "fsdp", None, None),
        P(),
        P(),
        P(),
    )
    out_specs = (P("dp", "fsdp", None, None), P("dp", "fsdp", None, None, None), P("fsdp", None))
    return jax.shard_map(
        per_device, mesh=mesh, in_specs=in_specs, out_specs=out_specs, check_vma=False
    )
```

profile of v0, /device:TPU:0, one launch (start us, length us, event | category | flops | bytes accessed | tf_op | source)
XLA Modules:
  0.0 448.5 jit_solution(8723042183354032274)
XLA Ops:
  8.6 5.8 %gather_fusion.2 = bf16[8,64,4992]{2,1,0:T(8,128)(2,1)} fusion(bf16[8,64,4992]{2,1,0:T(8,128)(2,1)} %bitcast.91, s32[1024]{0:T(1024)S(1)} %pad_clamp_fusion.5), kind=kCustom, calls=%fused_computation.clone | custom fusion | bytes 10223648 | tf_op jit(solution)/shard_map/jit(_take)/gather | solution.py:124
  14.4 5.3 %broadcast_select_fusion.2 = bf16[8,64,4992]{2,1,0:T(8,128)(2,1)} fusion(bf16[8,64,4992]{2,1,0:T(8,128)(2,1)} %gather_fusion.2, pred[8]{0:T(512)(128)(4,1)S(1)} %get-tuple-element.18), kind=kLoop, calls=%fused_computation.17 | loop fusion | flops 2555904 | bytes 10223624 | tf_op jit(solution)/shard_map/jit(_take)/select_n | solution.py:124
  19.7 7.0 %all-to-all-start = ((bf16[8,64,4992]{2,1,0:T(8,128)(2,1)}), bf16[8,64,4992]{2,1,0:T(8,128)(2,1)}, u32[]{:S(2)}, u32[]{:S(2)}) async-start(bf16[8,64,4992]{2,1,0:T(8,128)(2,1)} %broadcast_select_fusion.2), calls=%async_computation | async-start | bytes 10223616 | tf_op jit(solution)/shard_map/all_to_all | solution.py:125
  28.1 72.0 %all-to-all-done = bf16[8,64,4992]{2,1,0:T(8,128)(2,1)} async-done(((bf16[8,64,4992]{2,1,0:T(8,128)(2,1)}), bf16[8,64,4992]{2,1,0:T(8,128)(2,1)}, u32[]{:S(2)}, u32[]{:S(2)}) %all-to-all-start) | async-done | bytes 5111840 | tf_op jit(solution)/shard_map/all_to_all | solution.py:125
  100.1 5.9 %gather_fusion.3 = bf16[8,64,4992]{2,1,0:T(8,128)(2,1)} fusion(bf16[8,64,4992]{2,1,0:T(8,128)(2,1)} %all-to-all-done, s32[1024]{0:T(1024)S(1)} %pad_clamp_fusion.4), kind=kCustom, calls=%fused_computation.1.clone | custom fusion | bytes 10223648 | tf_op jit(solution)/shard_map/jit(_take)/gather | solution.py:126
  106.0 5.4 %broadcast_select_fusion.1 = bf16[8,64,4992]{2,1,0:T(8,128)(2,1)} fusion(bf16[8,64,4992]{2,1,0:T(8,128)(2,1)} %gather_fusion.3, pred[8]{0:T(512)(128)(4,1)S(1)} %compare_and_fusion.3), kind=kLoop, calls=%fused_computation.16 | loop fusion | flops 2555904 | bytes 10223624 | tf_op jit(solution)/shard_map/jit(_take)/select_n | solution.py:126
  111.5 12.5 %gather_fusion = bf16[320,4992]{1,0:T(8,128)(2,1)S(1)} fusion(bf16[512,4992]{1,0:T(8,128)(2,1)} %bitcast.88, s32[1024]{0:T(1024)S(1)} %pad_clamp_fusion.3), kind=kCustom, calls=%fused_computation.4 | custom fusion | bytes 6391040 | tf_op jit(solution)/shard_map/gather | solution.py:127
  130.9 3.5 reshape.318
  141.1 9.6 %convolution_convert_fusion = bf16[320,1664]{1,0:T(8,128)(2,1)} fusion(bf16[3200,1664]{1,0:T(8,128)(2,1)} %all-gather.2.cloned.1.call-done, bf16[1,1,320,3200]{3,2,1,0:T(8,128)(2,1)} %param.12, f32[3200]{0:T(1024)S(1)} %copy-done.12), kind=kOutput, calls=%fused_computation.29 | convolution fusion | flops 3411476480 | bytes 13775360 | tf_op jit(solution)/shard_map/dot_general | solution.py:132
  150.7 3.2 reshape.326
  153.9 4.7 %fusion.12 = (f32[320,13]{0,1:T(8,128)S(1)}, bf16[1,320,13,128]{3,1,2,0:T(8,128)(2,1)S(1)}) fusion(f32[1,320,13,128]{3,2,1,0:T(8,128)} %reshape.326, bf16[13,320,320]{1,2,0:T(8,128)(2,1)S(1)} %fusion.10, bf16[320,13,128]{2,1,0:T(8,128)(2,1)} %reshape.318, pred[320]{0:T(512)(128)(4,1)S(1)} %broadcast_compare_fusion.1), kind=kOutput, calls=%fused_computation.34 | convolution fusion | flops 343445440 | bytes 6939200 | tf_op jit(solution)/shard_map/bhqk,bkhd->bqhd/dot_general | solution.py:37
  160.4 10.3 %fusion.14 = f32[3200,1664]{1,0:T(8,128)} fusion(bf16[1,1,320,3200]{3,2,1,0:T(8,128)(2,1)S(1)} %copy-done.10, f32[3200]{0:T(1024)S(1)} %copy-done.12, bf16[40,8,13,128]{3,2,1,0:T(8,128)(2,1)S(1)} %bitcast.92), kind=kOutput, calls=%fused_computation.38 | convolution fusion | flops 3410944000 | bytes 24424960 | tf_op jit(solution)/shard_map/dot_general | solution.py:143
  173.6 4.1 multiply_convert_fusion
  181.2 5.0 %gather_fusion.1 = bf16[512,4992]{1,0:T(8,128)(2,1)} fusion(bf16[320,4992]{1,0:T(8,128)(2,1)S(1)} %maximum_bitcast_fusion, s32[1024]{0:T(1024)S(1)} %pad_clamp_fusion.2), kind=kCustom, calls=%fused_computation.5 | custom fusion | bytes 10225664 | tf_op jit(solution)/shard_map/gather | solution.py:137
  186.2 5.4 %broadcast_select_fusion.3 = bf16[8,64,4992]{2,1,0:T(8,128)(2,1)} fusion(bf16[8,64,4992]{2,1,0:T(8,128)(2,1)} %bitcast.89, pred[8,64]{1,0:T(8,128)(4,1)S(1)} %iota_compare_fusion.3), kind=kLoop, calls=%fused_computation.18 | loop fusion | flops 2555904 | bytes 10224128 | tf_op jit(solution)/shard_map/jit(_where)/select_n | solution.py:136
  191.6 5.9 %gather_fusion.4 = bf16[8,64,4992]{2,1,0:T(8,128)(2,1)} fusion(bf16[8,64,4992]{2,1,0:T(8,128)(2,1)} %broadcast_select_fusion.3, s32[1024]{0:T(1024)S(1)} %pad_clamp_fusion.1), kind=kCustom, calls=%fused_computation.2.clone | custom fusion | bytes 10223648 | tf_op jit(solution)/shard_map/jit(_take)/gather | solution.py:139
  197.5 5.5 %broadcast_select_fusion = bf16[8,64,4992]{2,1,0:T(8,128)(2,1)} fusion(bf16[8,64,4992]{2,1,0:T(8,128)(2,1)} %gather_fusion.4, pred[8]{0:T(512)(128)(4,1)S(1)} %get-tuple-element.17), kind=kLoop, calls=%fused_computation.15 | loop fusion | flops 2555904 | bytes 10223624 | tf_op jit(solution)/shard_map/jit(_take)/select_n | solution.py:139
  203.0 4.8 %all-to-all-start.1 = ((bf16[8,64,4992]{2,1,0:T(8,128)(2,1)}), bf16[8,64,4992]{2,1,0:T(8,128)(2,1)}, u32[]{:S(2)}, u32[]{:S(2)}) async-start(bf16[8,64,4992]{2,1,0:T(8,128)(2,1)} %broadcast_select_fusion), calls=%async_computation.1 | async-start | bytes 10223616 | tf_op jit(solution)/shard_map/all_to_all | solution.py:140
  207.9 11.8 %fusion.2 = bf16[1,1,320,3200]{3,2,1,0:T(8,128)(2,1)} fusion(bf16[3200,1664]{1,0:T(8,128)(2,1)} %all-gather.2.cloned.1.call-done, f32[3200]{0:T(1024)S(1)} %copy-done.12, bf16[40,8,13,128]{3,2,1,0:T(8,128)(2,1)S(1)} %bitcast.93), kind=kOutput, calls=%fused_computation.19 | convolution fusion | flops 3409920000 | bytes 13775360 | tf_op jit(solution)/shard_map/dot_general | solution.py:81
  219.7 58.9 %all-to-all-done.1 = bf16[8,64,4992]{2,1,0:T(8,128)(2,1)} async-done(((bf16[8,64,4992]{2,1,0:T(8,128)(2,1)}), bf16[8,64,4992]{2,1,0:T(8,128)(2,1)}, u32[]{:S(2)}, u32[]{:S(2)}) %all-to-all-start.1) | async-done | bytes 5111840 | tf_op jit(solution)/shard_map/all_to_all | solution.py:140
  278.6 5.9 %gather_fusion.5 = bf16[8,64,4992]{2,1,0:T(8,128)(2,1)} fusion(bf16[8,64,4992]{2,1,0:T(8,128)(2,1)} %all-to-all-done.1, s32[1024]{0:T(1024)S(1)} %pad_clamp_fusion), kind=kCustom, calls=%fused_computation.3.clone | custom fusion | bytes 10223648 | tf_op jit(solution)/shard_map/jit(_take)/gather | solution.py:141
  284.5 62.1 %reduce-scatter.5.cloned.1.call-done = f32[200,1664]{1,0:T(8,128)} async-done(((f32[3200,1664]{1,0:T(8,128)}), f32[200,1664]{1,0:T(8,128)}) %reduce-scatter.5.cloned.1.call-update) | async-done | bytes 1331216
  346.6 5.3 %select_bitcast_fusion = bf16[1,1,8,64,4992]{4,3,2,1,0:T(8,128)(2,1)} fusion(bf16[8,64,4992]{2,1,0:T(8,128)(2,1)} %gather_fusion.5, pred[8]{0:T(512)(128)(4,1)S(1)} %compare_and_fusion.1), kind=kLoop, calls=%fused_computation.14 | loop fusion | flops 2555904 | bytes 10223624 | tf_op jit(solution)/shard_map/broadcast_in_dim | solution.py:151
  352.0 87.5 %all-reduce.3.cloned.1.call-done = f32[200,1664]{1,0:T(8,128)} async-done(((f32[200,1664]{1,0:T(8,128)}), f32[200,1664]{1,0:T(8,128)}) %all-reduce.3.cloned.1.call-update) | async-done | bytes 1331216 | tf_op jit(solution)/shard_map/psum | solution.py:150
  (75 shorter events, 26.7 us)
Async XLA Ops:
  7.2 0.8 copy-start
  7.2 133.9 %all-gather.2.cloned.1.call-start = ((), (), s32[]{:S(2)}) async-start(), calls=%async_computation.3 | async-start | bytes 11315200 | tf_op jit(solution)/shard_map/all_gather | solution.py:123
  19.7 80.3 %all-to-all-start = ((bf16[8,64,4992]{2,1,0:T(8,128)(2,1)}), bf16[8,64,4992]{2,1,0:T(8,128)(2,1)}, u32[]{:S(2)}, u32[]{:S(2)}) async-start(bf16[8,64,4992]{2,1,0:T(8,128)(2,1)} %broadcast_select_fusion.2), calls=%async_computation | async-start | bytes 10223616 | tf_op jit(solution)/shard_map/all_to_all | solution.py:125
  26.8 319.8 %reduce-scatter.5.cloned.1.call-start = ((), (), s32[]{:S(2)}) async-start(), calls=%async_computation.5 | async-start | bytes 22630400
  128.1 7.4 %copy-start.2 = (bf16[320,13,128]{2,1,0:T(8,128)(2,1)}, bf16[320,13,128]{2,1,0:T(8,128)(2,1)S(1)}, u32[]{:S(2)}) copy-start(bf16[320,13,128]{2,1,0:T(8,128)(2,1)S(1)} %reshape.320) | copy-start | bytes 3194884
  130.9 4.6 %copy-start.8 = (bf16[320,13,128]{2,1,0:T(8,128)(2,1)}, bf16[320,13,128]{2,1,0:T(8,128)(2,1)S(1)}, u32[]{:S(2)}) copy-start(bf16[320,13,128]{2,1,0:T(8,128)(2,1)S(1)} %reshape.319) | copy-start | bytes 3194884
  137.6 2.7 copy-start.4
  140.3 0.7 copy-start.12
  153.9 6.5 %copy-start.10 = (bf16[1,1,320,3200]{3,2,1,0:T(8,128)(2,1)S(1)}, bf16[1,1,320,3200]{3,2,1,0:T(8,128)(2,1)}, u32[]{:S(2)}) copy-start(bf16[1,1,320,3200]{3,2,1,0:T(8,128)(2,1)} %param.12) | copy-start | bytes 6144004
  159.3 1.1 copy-start.5
  171.0 2.6 copy-start.7
  171.0 2.6 copy-start.11
  173.5 4.1 copy-start.9
  177.7 1.6 copy-start.3
  203.0 4.9 %copy-start.6 = (bf16[1,320,13,128]{3,2,1,0:T(8,128)(2,1)S(1)}, bf16[1,320,13,128]{3,2,1,0:T(8,128)(2,1)}, u32[]{:S(2)}) copy-start(bf16[1,320,13,128]{3,2,1,0:T(8,128)(2,1)} %copy-done.5) | copy-start | bytes 3194884
  203.0 75.6 %all-to-all-start.1 = ((bf16[8,64,4992]{2,1,0:T(8,128)(2,1)}), bf16[8,64,4992]{2,1,0:T(8,128)(2,1)}, u32[]{:S(2)}, u32[]{:S(2)}) async-start(bf16[8,64,4992]{2,1,0:T(8,128)(2,1)} %broadcast_select_fusion), calls=%async_computation.1 | async-start | bytes 10223616 | tf_op jit(solution)/shard_map/all_to_all | solution.py:140
  207.8 231.7 %all-reduce.3.cloned.1.call-start = ((), (), s32[]{:S(2)}) async-start(), calls=%async_computation.4 | async-start | bytes 2662400 | tf_op jit(solution)/shard_map/psum | solution.py:150
  346.6 95.4 %copy-start.1 = (s32[8,16,8]{1,2,0:T(8,128)S(1)}, s32[8,16,8]{1,2,0:T(8,128)}, u32[]{:S(2)}) copy-start(s32[8,16,8]{1,2,0:T(8,128)} %param.14) | copy-start | bytes 12292
Sparse Core Ops, SparseCore 0:
  9.7 119.8 all-gather.1
  170.8 175.6 reduce-scatter.4
  349.1 90.3 all-reduce.2
where the time goes:
time: 450 us; the launch traced here: 449 us
  waiting for transfers between devices  281 us (62%)
  local copies, waits for them, and re-layouts  64 us (14%)
  matrix products  46.4 us (10%)
  other arithmetic  30.8 us (7%)
  between operations  14.1 us (3%)
  starting transfers between devices  11.9 us (3%)
    psum x1, waiting for transfers between devices, per_device(): weight_grad = lax.psum(shard_sum, 'dp')  87.5 us
    all_to_all x1, waiting for transfers between devices, per_device(): lax.all_to_all(outgoing, 'dp', split_axis=0, concat_axis=0, tiled=True)  72 us
    unnamed x4, waiting for transfers between devices  62.8 us
    all_to_all x1, waiting for transfers between devices, per_device(): lax.all_to_all(back_send, 'dp', split_axis=0, concat_axis=0, tiled=True)  58.9 us
    gather x1, local copies, waits for them, and re-layouts, per_device(): block = images.reshape(images_count * slot_len, -1)[flat_index][None]  12.5 us
    dot_general x1, matrix products, project(): lax.dot_general(attended, weights, (((1,), (1,)), ((), ())), preferred_el...  11.8 us
    dot_general x1, matrix products, per_device(): lax.dot_general(scaled, attended, (((0,), (0,)), ((), ())), preferred_ele...  10.3 us
    dot_general x1, matrix products, per_device(): jnp.dot(scaled, weights, preferred_element_type=jnp.float32)  9.64 us
  transfers between devices with their start and end apart: 5, of which 4 were waited for; matrix products, arithmetic and copies ran while one was open for 24% of the time, Pallas kernels for 0%

commit v1 on v0

--- a/solution.py
+++ b/solution.py
@@ -98,56 +98,56 @@
     my_offsets = lax.dynamic_index_in_dim(col_offsets, dp_index, 0, keepdims=False)
     slot_data = qkv_rows[0, 0]
     grad_rows = out_grad[0, 0]
-    images_count = slot_data.shape[0]
-    slot_len = slot_data.shape[1]
+    images_count, slot_len = slot_data.shape[:2]
     own_rows = grad_rows.shape[0]
     slot_pos = jnp.arange(slot_len, dtype=jnp.int32)
     image_ids = jnp.arange(images_count, dtype=jnp.int32)
     owner_ids = jnp.arange(dp_count, dtype=jnp.int32)
     row_ids = jnp.arange(own_rows, dtype=jnp.int32)
-    matches = (col_plan == dp_index).astype(jnp.int32)
-    send_slot = jnp.sum(matches * image_ids[None, :], axis=1)
-    owner_of_slot = jnp.sum(matches * owner_ids[:, None], axis=0)
-    image_of_source = jnp.sum(
-        (my_plan[None, :] == owner_ids[:, None]).astype(jnp.int32) * image_ids[None, :], axis=1
+    slot_of_owner = col_plan == dp_index
+    loader_counts = jnp.sum(jnp.where(slot_of_owner, col_counts, 0), axis=0)
+    image_of_loader = my_plan[None, :] == owner_ids[:, None]
+    offset_from = jnp.sum(jnp.where(image_of_loader, my_offsets[None, :], 0), axis=1)
+    count_from = jnp.sum(jnp.where(image_of_loader, my_counts[None, :], 0), axis=1)
+    source_row = jnp.where(
+        slot_pos[None, :] < count_from[:, None], offset_from[:, None] + slot_pos[None, :], -1
+    ).reshape(-1)
+    pack = (row_ids[:, None] == source_row[None, :]).astype(jnp.bfloat16)
+    groups = jnp.where(slot_pos[None, :] < loader_counts[:, None], 0, -1)
+
+    weights = lax.all_gather(proj_weight, "fsdp", axis=0, tiled=True)
+    attn_out, soft, soft_low = attend(slot_data, groups)
+    swap = slot_of_owner.astype(jnp.bfloat16)
+    width = attn_out.shape[-1]
+    outgoing = jnp.dot(swap, attn_out.reshape(images_count, -1))
+    incoming = lax.all_to_all(
+        outgoing.reshape(dp_count, slot_len, width), "dp", split_axis=0, concat_axis=0, tiled=True
     )
-    inside = (
-        (row_ids[:, None] >= my_offsets[None, :])
-        & (row_ids[:, None] < (my_offsets + my_counts)[None, :])
-    ).astype(jnp.int32)
-    segment = jnp.sum(inside * image_ids[None, :], axis=1)
-    row_base = jnp.sum(inside * my_offsets[None, :], axis=1)
-    flat_index = segment * slot_len + row_ids - row_base
-    back_index = jnp.clip(my_offsets[:, None] + slot_pos[None, :], 0, own_rows - 1)
-    slot_valid = slot_pos[None, :] < my_counts[:, None]
-    weights = lax.all_gather(proj_weight, "fsdp", axis=0, tiled=True)
-    outgoing = jnp.take(slot_data, send_slot, axis=0)
-    incoming = lax.all_to_all(outgoing, "dp", split_axis=0, concat_axis=0, tiled=True)
-    images = jnp.take(incoming, my_plan, axis=0)
-    block = images.reshape(images_count * slot_len, -1)[flat_index][None]
-    attn_out, soft, soft_low = attend(block, segment[None])
-    attended = attn_out[0]
-    branch_rows = project(attended, weights, layer_scale)
+    attended = jnp.dot(pack, incoming.reshape(-1, width))
     scaled = (grad_rows.astype(jnp.float32) * layer_scale).astype(jnp.bfloat16)
     grad_attended = jnp.dot(scaled, weights, preferred_element_type=jnp.float32).astype(
         jnp.bfloat16
     )
-    grad_block = attend_back(block, soft, soft_low, attn_out, grad_attended[None])[0]
-    grad_slots = jnp.where(
-        slot_valid[..., None], grad_block[back_index], jnp.zeros((), jnp.bfloat16)
+    back_send = jnp.dot(pack.T, grad_attended)
+    returned = lax.all_to_all(
+        back_send.reshape(dp_count, slot_len, width), "dp", split_axis=0, concat_axis=0, tiled=True
     )
-    back_send = jnp.take(grad_slots, image_of_source, axis=0)
-    returned = lax.all_to_all(back_send, "dp", split_axis=0, concat_axis=0, tiled=True)
-    grad_patches = jnp.take(returned, owner_of_slot, axis=0)
+    grad_slots = jnp.dot(swap.T, returned.reshape(dp_count, -1)).reshape(
+        images_count, slot_len, width
+    )
+    branch_rows = project(attended, weights, layer_scale)
     shard_sum = lax.psum_scatter(
         lax.dot_general(
             scaled, attended, (((0,), (0,)), ((), ())), preferred_element_type=jnp.float32
-        ),
+        ).astype(jnp.bfloat16),
         "fsdp",
         scatter_dimension=0,
         tiled=True,
     )
-    weight_grad = lax.psum(shard_sum, "dp")
+    weight_grad = lax.psum(shard_sum.astype(jnp.float32), "dp")
+    grad_patches = attend_back(slot_data, soft, soft_low, attn_out, grad_slots)
+    valid = slot_pos[None, :] < loader_counts[:, None]
+    grad_patches = jnp.where(valid[..., None], grad_patches, jnp.zeros((), jnp.bfloat16))
     return (branch_rows[None, None], grad_patches[None, None], weight_grad)
 
 

time: 450 us -> 360 us (0.80)
  waiting for transfers between devices: 281 us -> 130 us
  blocking collectives: 0 us -> 116 us
  local copies, waits for them, and re-layouts: 64 us -> 32.7 us
  other arithmetic: 30.8 us -> 8.8 us
  starting transfers between devices: 11.9 us -> 6.96 us
  matrix products: 46.4 us -> 51 us
    all_to_all x2 -> x1, waiting for transfers between devices: 131 us -> 16.6 us  [per_device(): lax.all_to_all(back_send.reshape(dp_count, slot_len, width), 'dp', split_...]
    psum x0 -> x1, blocking collectives: none -> 88.9 us  [per_device(): weight_grad = lax.psum(shard_sum.astype(jnp.float32), 'dp')]
    psum x1 -> x0, waiting for transfers between devices: 87.5 us -> none  [per_device(): weight_grad = lax.psum(shard_sum, 'dp')]
    all_gather x1, waiting for transfers between devices: 0.02 us -> 63.8 us  [per_device(): weights = lax.all_gather(proj_weight, 'fsdp', axis=0, tiled=True)]
    gather x6 -> x0, local copies, waits for them, and re-layouts: 41.1 us -> none  [the longest x1 12.5 us: per_device(): block = images.reshape(images_count * slot_len, -1)[flat_index][None]]
    all_to_all x0 -> x1, blocking collectives: none -> 26.6 us  [per_device(): lax.all_to_all(outgoing.reshape(dp_count, slot_len, width), 'dp', split_a...]
    select_n x9 -> x3, other arithmetic: 21.7 us -> 4.97 us  [the longest x1 4.82 us: per_device(): jnp.where(valid[..., None], grad_patches, jnp.zeros((), jnp.bfloat16))]
    unnamed x4 -> x3, waiting for transfers between devices: 62.8 us -> 49.5 us
  transfers between devices with their start and end apart: 5 -> 3, of which waited for: 4 -> 3; matrix products, arithmetic and copies ran while one was open for 24% -> 15% of each run, Pallas kernels for 0% -> 0%
where the time goes in v1:
time: 360 us; the launch traced here: 359 us
  waiting for transfers between devices  130 us (36%)
  blocking collectives  116 us (32%)
  matrix products  51 us (14%)
  local copies, waits for them, and re-layouts  32.7 us (9%)
  between operations  14.2 us (4%)
  other arithmetic  8.8 us (2%)
  starting transfers between devices  6.96 us (2%)
    psum x1, blocking collectives, per_device(): weight_grad = lax.psum(shard_sum.astype(jnp.float32), 'dp')  88.9 us
    all_gather x1, waiting for transfers between devices, per_device(): weights = lax.all_gather(proj_weight, 'fsdp', axis=0, tiled=True)  63.8 us
    unnamed x3, waiting for transfers between devices  49.5 us
    all_to_all x1, blocking collectives, per_device(): lax.all_to_all(outgoing.reshape(dp_count, slot_len, width), 'dp', split_a...  26.6 us
    all_to_all x1, waiting for transfers between devices, per_device(): lax.all_to_all(back_send.reshape(dp_count, slot_len, width), 'dp', split_...  16.6 us
    dot_general x1, matrix products, project(): lax.dot_general(attended, weights, (((1,), (1,)), ((), ())), preferred_el...  11.5 us
    dot_general x1, matrix products, per_device(): back_send = jnp.dot(pack.T, grad_attended)  11.4 us
    concatenate x3, local copies, waits for them, and re-layouts, attend_back(): jnp.concatenate([grad_query.reshape(shape_lead + (width_all,)), grad_key....  10.6 us
  transfers between devices with their start and end apart: 3, of which 3 were waited for; matrix products, arithmetic and copies ran while one was open for 15% of the time, Pallas kernels for 0%

profile of v1, /device:TPU:0, one launch (start us, length us, event | category | flops | bytes accessed | tf_op | source)
XLA Modules:
  0.0 359.2 jit_solution(14074739035321660243)
XLA Ops:
  11.2 63.8 %all-gather.2.cloned.1.call-done = bf16[3200,1664]{1,0:T(8,128)(2,1)} async-done(((bf16[200,1664]{1,0:T(8,128)(2,1)}), bf16[3200,1664]{1,0:T(8,128)(2,1)}) %all-gather.2.cloned.1.call-update) | async-done | bytes 10649616 | tf_op jit(solution)/shard_map/all_gather | solution.py:118
  75.0 11.4 %fusion.37 = bf16[512,1664]{1,0:T(8,128)(2,1)} fusion(bf16[3200,1664]{1,0:T(8,128)(2,1)} %all-gather.2.cloned.1.call-done, bf16[1,1,320,3200]{3,2,1,0:T(8,128)(2,1)} %param.10, f32[3200]{0:T(1024)} %param.9, s32[512]{0:T(512)S(1)} %select_n.85), kind=kOutput, calls=%fused_computation.45 | convolution fusion | flops 3956899840 | bytes 14416384 | tf_op jit(solution)/shard_map/dot_general | solution.py:131
  86.4 6.7 %all-to-all-start.1 = ((bf16[8,64,1664]{2,1,0:T(8,128)(2,1)}), bf16[8,64,1664]{2,1,0:T(8,128)(2,1)}, u32[]{:S(2)}, u32[]{:S(2)}) async-start(bf16[8,64,1664]{2,1,0:T(8,128)(2,1)} %bitcast.10), calls=%async_computation.1 | async-start | bytes 3407872 | tf_op jit(solution)/shard_map/all_to_all | solution.py:132
  93.6 4.8 %slice_bitcast_fusion.2 = (bf16[8,8,13,8,128]{4,3,2,1,0:T(8,128)(2,1)S(1)}, bf16[8,8,13,8,128]{4,3,2,1,0:T(8,128)(2,1)}, bf16[8,8,13,8,128]{4,3,2,1,0:T(8,128)(2,1)S(1)}) fusion(bf16[8,64,4992]{2,1,0:T(8,128)(2,1)} %bitcast.79), kind=kLoop, calls=%fused_computation.27 | loop fusion | bytes 10223616
  99.4 3.4 fusion.50
  102.8 16.6 %all-to-all-done.1 = bf16[8,64,1664]{2,1,0:T(8,128)(2,1)} async-done(((bf16[8,64,1664]{2,1,0:T(8,128)(2,1)}), bf16[8,64,1664]{2,1,0:T(8,128)(2,1)}, u32[]{:S(2)}, u32[]{:S(2)}) %all-to-all-start.1) | async-done | bytes 1703968 | tf_op jit(solution)/shard_map/all_to_all | solution.py:132
  119.4 2.7 fusion.42
  122.2 4.3 %multiply_reduce_fusion = (f32[8,64,13]{1,2,0:T(8,128)S(1)}, bf16[8,64,13,128]{3,1,2,0:T(8,128)(2,1)S(1)}) fusion(bf16[8,64,13,128]{3,0,2,1:T(8,128)(2,1)S(1)} %fusion.42, bf16[8,8,13,8,128]{4,3,2,1,0:T(8,128)(2,1)S(1)} %copy-done.2, f32[8,13,64,64]{2,3,1,0:T(8,128)} %get-tuple-element.13, f32[8,13,64]{2,1,0:T(8,128)S(1)} %copy-done.8, ...), kind=kOutput, calls=%fused_computation.11 | convolution fusion | flops 115009024 | bytes 6869504 | tf_op jit(solution)/shard_map/bhqk,bkhd->bqhd/dot_general | solution.py:37
  126.5 2.5 copy.65
  129.0 3.9 %reshape_reshape.4 = bf16[8,106496]{1,0:T(8,128)(2,1)} reshape(bf16[8,64,13,128]{3,2,1,0:T(8,128)(2,1)} %copy.65) | data formatting | bytes 3407872 | tf_op jit(solution)/shard_map/reshape;reshape | solution.py:122
  132.9 2.0 fusion.44
  135.2 26.6 %all_to_all.10 = bf16[8,64,1664]{2,1,0:T(8,128)(2,1)S(1)} all-to-all(bf16[8,64,1664]{2,1,0:T(8,128)(2,1)S(1)} %copy.66), channel_id=1, replica_groups=mesh['dp'=8,'fsdp'=16] {'dp'}, dimensions={0} | all-to-all | bytes 3407872 | tf_op jit(solution)/shard_map/all_to_all | solution.py:123
  163.6 8.7 %convolution_convert_fusion = bf16[3200,1664]{1,0:T(8,128)(2,1)} fusion(bf16[320,1664]{1,0:T(8,128)(2,1)S(1)} %fusion.39, bf16[1,1,320,3200]{3,2,1,0:T(8,128)(2,1)S(1)} %copy-done.4, f32[3200]{0:T(1024)S(1)} %copy-done.5), kind=kOutput, calls=%fused_computation.1 | convolution fusion | flops 3416268800 | bytes 13775360 | tf_op jit(solution)/shard_map/dot_general | solution.py:140
  172.3 3.2 fusion.17
  175.5 2.6 copy.78
  178.1 4.2 %concatenate.18 = bf16[1,1,8,64,1664]{4,3,2,1,0:T(8,128)(2,1)} reshape(bf16[8,64,13,128]{3,2,1,0:T(8,128)(2,1)} %copy.78) | data formatting | bytes 3407872 | tf_op jit(solution)/shard_map/concatenate | solution.py:70
  182.2 4.0 %multiply_convert_fusion.2 = bf16[8,13,64,64]{2,3,1,0:T(8,128)(2,1)S(1)} fusion(f32[8,13,64]{2,1,0:T(8,128)S(1)} %bitcast.81, bf16[8,8,13,8,128]{4,3,2,1,0:T(8,128)(2,1)} %get-tuple-element.8, f32[8,13,64,64]{2,3,1,0:T(8,128)} %get-tuple-element.13, f32[8,13,64]{2,1,0:T(8,128)} %get-tuple-element.12, bf16[8,64,13,128]{3,0,2,1:T(8,128)(2,1)} %copy-done.3), kind=kOutput, calls=%fused_computation.10 | convolution fusion | flops 110755840 | bytes 6017024 | tf_op jit(solution)/shard_map/bqhd,bkhd->bhqk/dot_general | solution.py:55
  187.5 2.5 copy.76
  190.0 4.3 %concatenate.17 = bf16[1,1,8,64,1664]{4,3,2,1,0:T(8,128)(2,1)} reshape(bf16[8,64,13,128]{3,2,1,0:T(8,128)(2,1)} %copy.76) | data formatting | bytes 3407872 | tf_op jit(solution)/shard_map/concatenate | solution.py:70
  196.2 2.1 concatenate.16
  198.3 4.8 %maximum_select_fusion = bf16[1,1,8,64,4992]{4,3,2,1,0:T(8,128)(2,1)} fusion(bf16[1,1,8,64,1664]{4,3,2,1,0:T(8,128)(2,1)} %concatenate.18, bf16[1,1,8,64,1664]{4,3,2,1,0:T(8,128)(2,1)} %concatenate.17, bf16[1,1,8,64,1664]{4,3,2,1,0:T(8,128)(2,1)} %concatenate.16, pred[8,64]{1,0:T(8,128)(4,1)S(1)} %get-tuple-element.10), kind=kLoop, calls=%fused_computation.4 | loop fusion | flops 17891328 | bytes 10224128 | tf_op jit(solution)/shard_map/jit(_where)/select_n | solution.py:150
  203.1 11.5 %fusion.2 = bf16[1,1,320,3200]{3,2,1,0:T(8,128)(2,1)} fusion(bf16[320,1664]{1,0:T(8,128)(2,1)S(1)} %copy-done.7, bf16[3200,1664]{1,0:T(8,128)(2,1)} %all-gather.2.cloned.1.call-done, f32[3200]{0:T(1024)S(1)} %copy-done.5), kind=kOutput, calls=%fused_computation.5 | convolution fusion | flops 3409920000 | bytes 13775360 | tf_op jit(solution)/shard_map/dot_general | solution.py:81
  214.6 48.8 %reduce-scatter.5.cloned.1.call-done = bf16[200,1664]{1,0:T(8,128)(2,1)} async-done(((bf16[3200,1664]{1,0:T(8,128)(2,1)}), bf16[200,1664]{1,0:T(8,128)(2,1)}) %reduce-scatter.5.cloned.1.call-update) | async-done | bytes 665616
  263.5 88.9 %all-reduce.2 = f32[200,1664]{1,0:T(8,128)} all-reduce(bf16[200,1664]{1,0:T(8,128)(2,1)} %reduce-scatter.5.cloned.1.call-done), channel_id=1, replica_groups=mesh['dp'=8,'fsdp'=16] {'dp'}, use_global_device_ids=true, to_apply=%region_7.8 | all-reduce | flops 332800 | bytes 1996800 | tf_op jit(solution)/shard_map/psum | solution.py:147
  (40 shorter events, 10.5 us)
Async XLA Ops:
  7.2 67.9 %all-gather.2.cloned.1.call-start = ((), (), s32[]{:S(2)}) async-start(), calls=%async_computation.3 | async-start | bytes 11315200 | tf_op jit(solution)/shard_map/all_gather | solution.py:118
  86.4 33.0 %all-to-all-start.1 = ((bf16[8,64,1664]{2,1,0:T(8,128)(2,1)}), bf16[8,64,1664]{2,1,0:T(8,128)(2,1)}, u32[]{:S(2)}, u32[]{:S(2)}) async-start(bf16[8,64,1664]{2,1,0:T(8,128)(2,1)} %bitcast.10), calls=%async_computation.1 | async-start | bytes 3407872 | tf_op jit(solution)/shard_map/all_to_all | solution.py:132
  93.1 170.3 %reduce-scatter.5.cloned.1.call-start = ((), (), s32[]{:S(2)}) async-start(), calls=%async_computation.4 | async-start | bytes 11315200
  119.4 2.7 copy-start.2
  119.4 2.7 copy-start.8
  122.1 4.3 %copy-start.3 = (bf16[8,64,13,128]{3,0,2,1:T(8,128)(2,1)}, bf16[8,64,13,128]{3,0,2,1:T(8,128)(2,1)S(1)}, u32[]{:S(2)}) copy-start(bf16[8,64,13,128]{3,0,2,1:T(8,128)(2,1)S(1)} %fusion.42) | copy-start | bytes 5111812
  161.8 1.8 copy-start.4
  161.8 1.8 copy-start.5
  162.6 1.0 copy-start.6
  186.3 1.2 copy-start
  190.0 4.3 %copy-start.1 = (bf16[8,13,64,64]{2,3,1,0:T(8,128)(2,1)S(1)}, bf16[8,13,64,64]{2,3,1,0:T(8,128)(2,1)}, u32[]{:S(2)}) copy-start(bf16[8,13,64,64]{2,3,1,0:T(8,128)(2,1)} %copy-done) | copy-start | bytes 2555908
  198.3 4.8 %copy-start.7 = (bf16[320,1664]{1,0:T(8,128)(2,1)S(1)}, bf16[320,1664]{1,0:T(8,128)(2,1)}, u32[]{:S(2)}) copy-start(bf16[320,1664]{1,0:T(8,128)(2,1)} %copy-done.6) | copy-start | bytes 3194884
Sparse Core Ops, SparseCore 0:
  9.7 65.2 all-gather.1
  172.4 91.0 reduce-scatter.4

commit v2 on v1

v2 whole, which is shorter than its diff:
```python
import math

import jax
import jax.numpy as jnp
from jax import lax
from jax.experimental import pallas as pl
from jax.experimental.pallas import tpu as pltpu
from jax.sharding import PartitionSpec as P

HEADS = 13
HEAD = 128
WIDTH = HEADS * HEAD
D = 3200
IMGS = 8
MAXP = 64
OWN = 320
SHARD = 200
PADDED = 208
HALF = 8 * PADDED
BLOCK = 896
SECOND = WIDTH - BLOCK
CUT = 96
MASKED = -1e30
MESH = pl.DeviceIdType.MESH
INV_SCALE = 1.0 / math.sqrt(HEAD)
F32 = jnp.float32
BF16 = jnp.bfloat16

NN = (((1,), (0,)), ((), ()))
NT = (((1,), (1,)), ((), ()))
TN = (((0,), (0,)), ((), ()))


def mm(a, b, dims=NN):
    return lax.dot_general(a, b, dims, preferred_element_type=F32)


def by_columns(body):
    @pl.loop(0, WIDTH // 256)
    def _(n):
        body(pl.multiple_of(n * 256, 128), 256)

    body(WIDTH - WIDTH % 256, WIDTH % 256)


def spread_tile(tile):
    first = tile * 128
    group = first // PADDED
    inside = first % PADDED
    start = lax.min((group * SHARD + lax.min(inside, SHARD)) // 128, D // 128 - 2)
    place = first + lax.broadcasted_iota(jnp.int32, (256, 128), 1)
    source = start * 128 + lax.broadcasted_iota(jnp.int32, (256, 128), 0)
    groups = group + (place >= (group + 1) * PADDED).astype(jnp.int32)
    local = place - groups * PADDED
    hit = (source == groups * SHARD + local) & (local < SHARD)
    return start * 128, jnp.where(hit, 1.0, 0.0).astype(BF16)


def compact_tile(tile):
    first = tile * 128
    group = first // SHARD
    start = lax.min((first + group * (PADDED - SHARD)) // 128, 2 * HALF // 128 - 3)
    place = first + lax.broadcasted_iota(jnp.int32, (384, 128), 1)
    source = start * 128 + lax.broadcasted_iota(jnp.int32, (384, 128), 0)
    groups = group + (place >= (group + 1) * SHARD).astype(jnp.int32)
    hit = source == place + groups * (PADDED - SHARD)
    return start * 128, jnp.where(hit, 1.0, 0.0).astype(BF16)


def fused(
    meta, shard_hbm, qkv_hbm, grad_hbm, scale, scale_pad, source_row, source_col,
    branch_hbm, qkv_grad_hbm, weight_grad_hbm,
    wv, wp, wh, qkv, sc, sp, sx, att_send, att_recv, aa, soft_keep,
    gh, relay, direct, total, relay2, direct2, summed, ysum, mixed, final, wout,
    ga_own, ga_send, ga_recv, back_send, back_recv, bp, bx,
    in_sem, w0s, w0r, w1s, w1r, a2s, a2r, cs, cr, g1s, g1r, g2s, g2r, ys, yr, fs, fr, b2s, b2r, out_sem,
):
    d = lax.axis_index("dp")
    f = lax.axis_index("fsdp")
    c = f % 2
    z = (f // 2) % 4
    yl = f // 8
    x = d // 2
    y = (d % 2) * 2 + yl

    def at(px, py, pz, pc):
        px, py, pz = (px + 4) % 4, (py + 4) % 4, (pz + 4) % 4
        return (px * 2 + py // 2, ((py % 2) * 4 + pz) * 2 + pc)

    def remote(src, dst, send, recv, dev):
        return pltpu.make_async_remote_copy(
            src_ref=src, dst_ref=dst, send_sem=send, recv_sem=recv, device_id=dev, device_id_type=MESH
        )

    partner = at(x, y, z, 1 - c)

    load_w = pltpu.make_async_copy(shard_hbm, wv, in_sem.at[0])
    load_q = pltpu.make_async_copy(qkv_hbm, qkv, in_sem.at[1])
    load_g = pltpu.make_async_copy(grad_hbm, sc, in_sem.at[2])
    load_w.start()
    load_q.start()
    load_g.start()

    barrier = pltpu.get_barrier_semaphore()
    peers = []
    for step in range(1, 8):
        other = (d + step) % 8
        peers += [(other, f), (other, f + 1 - 2 * c)]
    peers += [partner, at(x, y, z + 1, c), at(x, y, z - 1, c)]
    for sign in (1, -1):
        peers += [at(x, y + sign, z, 0), at(x, y + sign, z, 1)]
    for peer in peers:
        pl.semaphore_signal(barrier, inc=1, device_id=peer, device_id_type=MESH)
    load_w.wait()
    wp[0:192, :] = wv[0:192, :]
    wp[192:208, :] = jnp.concatenate(
        [wv[192:200, :].astype(F32), jnp.zeros((8, WIDTH), F32)], axis=0
    ).astype(BF16)
    pl.semaphore_wait(barrier, len(peers))

    def w_rows(pz, k):
        return wh.at[pl.ds(pl.multiple_of((((pz + 4) % 4) * 2 + k) * PADDED, 16), PADDED), :]

    w_y = remote(wp, w_rows(z, c), w0s.at[0], w0r.at[c], at(x, y + 1 - 2 * c, z, yl))
    w_c = remote(wp, w_rows(z, c), w0s.at[1], w0r.at[c], partner)
    w_l = pltpu.make_async_copy(wp, w_rows(z, c), w0s.at[1])
    w_y.start()

    @pl.when(c == yl)
    def _():
        w_l.start()

    @pl.when(c != yl)
    def _():
        w_c.start()

    load_q.wait()

    def att_copy(i):
        owner = (d + 1 + i) % 8
        return remote(att_send.at[owner], att_recv.at[d], a2s.at[i], a2r.at[i], (owner, f))

    @pl.loop(0, IMGS)
    def _(i):
        owner = (d + 1 + i) % 8
        slot = meta[0, owner]
        count = meta[1, owner]
        live = lax.broadcasted_iota(jnp.int32, (MAXP, MAXP), 1) < count
        for h in range(HEADS):
            cols = slice(h * HEAD, (h + 1) * HEAD)
            q = qkv[slot, :, cols]
            k = qkv[slot, :, WIDTH + h * HEAD : WIDTH + (h + 1) * HEAD]
            v = qkv[slot, :, 2 * WIDTH + h * HEAD : 2 * WIDTH + (h + 1) * HEAD]
            s = jnp.where(live, mm(q, k, NT) * INV_SCALE, MASKED)
            e = jnp.exp(s - jnp.max(s, axis=-1, keepdims=True))
            soft = e / jnp.sum(e, axis=-1, keepdims=True)
            soft_keep[owner, h] = soft
            att_send[owner, :, cols] = mm(soft.astype(BF16), v).astype(BF16)

        @pl.when(i < 7)
        def _():
            att_copy(i).start()

    att_recv[d] = att_send[d]

    for k in range(2):
        @pl.when((c != yl) | (c != k))
        def _():
            remote(wp, w_rows(z, k), w0s.at[0], w0r.at[k], partner).wait_recv()

    @pl.when(c == yl)
    def _():
        w_l.wait()

    up, down = at(x, y, z + 1, c), at(x, y, z - 1, c)
    w1 = [
        remote(w_rows(z, 0), w_rows(z, 0), w1s.at[0], w1r.at[0], up),
        remote(w_rows(z, 1), w_rows(z, 1), w1s.at[1], w1r.at[1], down),
        remote(w_rows(z, 1), w_rows(z, 1), w1s.at[2], w1r.at[2], up),
        remote(w_rows(z, 0), w_rows(z, 0), w1s.at[3], w1r.at[3], down),
    ]
    for copy in w1:
        copy.start()
    w2 = [
        remote(w_rows(z - 1, 0), w_rows(z - 1, 0), w1s.at[4], w1r.at[4], up),
        remote(w_rows(z + 1, 1), w_rows(z + 1, 1), w1s.at[5], w1r.at[5], down),
    ]

    load_g.wait()

    @pl.loop(0, OWN // 16)
    def _(r):
        rows = pl.ds(pl.multiple_of(r * 16, 16), 16)
        sc[rows, :] = (sc[rows, :].astype(F32) * scale[...]).astype(BF16)

    own_rows = pl.ds(pl.multiple_of(c * OWN, 16), OWN)
    other_rows = pl.ds(pl.multiple_of((1 - c) * OWN, 16), OWN)

    @pl.loop(0, HALF // 128)
    def _(t):
        start, pick = spread_tile((1 - c) * (HALF // 128) + t)
        window = sc[:, pl.ds(pl.multiple_of(start, 128), 256)]
        sx[:, pl.ds(pl.multiple_of(t * 128, 128), 128)] = mm(window, pick).astype(BF16)

    send_sx = remote(sx, sp.at[own_rows, :], cs.at[0], cr.at[0], partner)
    send_sx.start()

    @pl.loop(0, HALF // 128)
    def _(t):
        start, pick = spread_tile(c * (HALF // 128) + t)
        window = sc[:, pl.ds(pl.multiple_of(start, 128), 256)]
        sp[own_rows, pl.ds(pl.multiple_of(t * 128, 128), 128)] = mm(window, pick).astype(BF16)

    for i in range(7):
        source = (d + 7 - i) % 8
        remote(att_send.at[source], att_recv.at[source], a2s.at[i], a2r.at[i], partner).wait_recv()
    pack = jnp.where(
        lax.broadcasted_iota(jnp.int32, (OWN, IMGS * MAXP), 0) == source_row[...], 1.0, 0.0
    ).astype(BF16)

    def pack_columns(start, size):
        got = att_recv[:, :, pl.ds(start, size)].reshape(IMGS * MAXP, size)
        aa[own_rows, pl.ds(start, size)] = mm(pack, got).astype(BF16)

    by_columns(pack_columns)
    send_aa = remote(aa.at[own_rows, :], aa.at[own_rows, :], cs.at[1], cr.at[1], partner)
    send_aa.start()
    remote(sx, sp.at[other_rows, :], cs.at[0], cr.at[0], partner).wait_recv()
    remote(aa.at[other_rows, :], aa.at[other_rows, :], cs.at[1], cr.at[1], partner).wait_recv()

    @pl.loop(0, HALF // 128)
    def _(t):
        rows = pl.ds(pl.multiple_of(t * 128, 128), 128)
        part = mm(sp[:, rows], aa[...], TN)
        gh[0, rows, :] = part[:, :BLOCK].astype(BF16)
        gh[1, rows, :] = part[:, SECOND:].astype(BF16)

    def block(first, second):
        first, second = (first + 4) % 4, (second + 4) % 4
        pz = first * (1 - c) + second * c
        kh = second * (1 - c) + first * c
        return kh % 2, pl.ds(pl.multiple_of((pz * 2 + kh // 2) * PADDED, 16), PADDED)

    p1 = z * (1 - c) + x * c
    p2 = x * (1 - c) + z * c
    right1, left1 = at(x + c, y, z + 1 - c, c), at(x - c, y, z - 1 + c, c)
    right2, left2 = at(x + 1 - c, y, z + c, c), at(x - 1 + c, y, z - c, c)

    def g1(first, j, dst, sem, dev):
        h, rows = block(first, j)
        return remote(gh.at[h, rows, :], dst, g1s.at[sem], g1r.at[sem], dev)

    s1 = [g1(p1 + 2, j, relay.at[0, j], j, right1) for j in (0, 1)]
    s1 += [g1(p1 + 2, j, relay.at[1, j - 2], j, left1) for j in (2, 3)]
    s1 += [g1(p1 + 1, j, direct.at[0, j], 4 + j, right1) for j in (2, 3)]
    s1 += [g1(p1 - 1, j, direct.at[1, j], 8 + j, left1) for j in (0, 1)]
    for copy in (s1[0], s1[2], s1[1], s1[3], s1[4], s1[6], s1[5], s1[7]):
        copy.start()
    r1 = [g1(p1 + 1, j, direct.at[0, j], 4 + j, right1) for j in (0, 1)]
    r1 += [g1(p1 - 1, j, direct.at[1, j], 8 + j, left1) for j in (2, 3)]

    w1[0].wait_recv()
    w2[0].start()
    w1[1].wait_recv()
    w2[1].start()

    def add_rows(rows, body):
        @pl.loop(0, rows // 16)
        def _(r):
            body(pl.multiple_of(r * 16, 16))

    for n, j in enumerate((0, 2, 1, 3)):
        side, place = (0, p1 + 1) if j < 2 else (1, p1 - 1)
        s1[j].wait_recv()
        h, rows = block(place, j)
        base = rows.start

        def add_relay(r, h=h, base=base, side=side, j=j):
            here = pl.ds(pl.multiple_of(base + r, 16), 16)
            gh[h, here, :] = (
                gh[h, here, :].astype(F32) + relay[side, j % 2, pl.ds(r, 16), :].astype(F32)
            ).astype(BF16)

        add_rows(PADDED, add_relay)
        r1[j].start()

    w1[2].wait_recv()
    w1[3].wait_recv()
    w2[0].wait_recv()
    w2[1].wait_recv()

    def grad_columns(start, size):
        cols = pl.ds(start, size)
        ga_send[:, cols] = mm(sp[other_rows, :], wh[:, cols])
        ga_own[:, cols] = mm(sp[own_rows, :], wh[:, cols])

    by_columns(grad_columns)
    send_ga = remote(ga_send, ga_recv, cs.at[2], cr.at[2], partner)
    send_ga.start()
    send_ga.wait_recv()
    unpack = jnp.where(
        lax.broadcasted_iota(jnp.int32, (IMGS * MAXP, OWN), 1) == source_col[...], 1.0, 0.0
    ).astype(BF16)

    def unpack_columns(start, size):
        cols = pl.ds(start, size)
        grad = (ga_own[:, cols] + ga_recv[:, cols]).astype(BF16)
        back_send[:, :, cols] = mm(unpack, grad).astype(BF16).reshape(IMGS, MAXP, size)

    by_columns(unpack_columns)

    def back_copy(i):
        loader = (d + 1 + i) % 8
        return remote(back_send.at[loader], back_recv.at[d], b2s.at[i], b2r.at[i], (loader, f))

    for i in range(7):
        back_copy(i).start()
    back_recv[d] = back_send[d]

    for j in range(4):
        (s1[4 + j - 2] if j >= 2 else r1[j]).wait_recv()
        (s1[6 + j] if j < 2 else r1[j]).wait_recv()
        h, rows = block(p1, j)
        base = rows.start

        def add_first(r, h=h, base=base, j=j):
            here = pl.ds(r, 16)
            total[j, here, :] = (
                gh[h, pl.ds(pl.multiple_of(base + r, 16), 16), :].astype(F32)
                + direct[0, j, here, :].astype(F32)
                + direct[1, j, here, :].astype(F32)
            ).astype(BF16)

        add_rows(PADDED, add_first)

    low, high = pl.ds(0, CUT), pl.ds(CUT, PADDED - CUT)

    def g2(place, rows, dst, sem, dev):
        return remote(total.at[(place + 4) % 4, rows, :], dst, g2s.at[sem], g2r.at[sem], dev)

    s2 = [
        g2(p2 + 2, low, relay2.at[low, :], 0, right2),
        g2(p2 + 2, high, relay2.at[high, :], 1, left2),
        g2(p2 + 1, high, direct2.at[0, high, :], 2, right2),
        g2(p2 - 1, low, direct2.at[1, low, :], 3, left2),
    ]
    r2 = [
        g2(p2 + 1, low, direct2.at[0, low, :], 4, right2),
        g2(p2 - 1, high, direct2.at[1, high, :], 5, left2),
    ]
    for copy in s2:
        copy.start()

    @pl.loop(0, HALF // 128)
    def _(t):
        rows = pl.ds(pl.multiple_of(t * 128, 128), 128)
        there = pl.ds(pl.multiple_of(c * HALF + t * 128, 128), 128)
        factor = scale_pad[:, there]
        weights = wh[rows, :]
        bx[:, rows] = (factor * mm(aa[other_rows, :], weights, NT)).astype(BF16)
        bp[:, there] = (factor * mm(aa[own_rows, :], weights, NT)).astype(BF16)

    my_half = bp.at[:, pl.ds(pl.multiple_of(c * HALF, 128), HALF)]
    other_half = bp.at[:, pl.ds(pl.multiple_of((1 - c) * HALF, 128), HALF)]
    send_bx = remote(bx, my_half, cs.at[3], cr.at[3], partner)
    send_bx.start()

    for side in range(2):
        s2[side].wait_recv()
        place = (p2 + 1 if side == 0 else p2 + 3) % 4
        offset, rows = (0, CUT) if side == 0 else (CUT, PADDED - CUT)

        def add_relay2(r, place=place, offset=offset):
            here = pl.ds(pl.multiple_of(offset + r, 16), 16)
            total[place, here, :] = (
                total[place, here, :].astype(F32) + relay2[here, :].astype(F32)
            ).astype(BF16)

        add_rows(rows, add_relay2)
        r2[side].start()

    remote(bx, other_half, cs.at[3], cr.at[3], partner).wait_recv()

    @pl.loop(0, D // 128)
    def _(t):
        start, pick = compact_tile(t)
        window = bp[:, pl.ds(pl.multiple_of(start, 128), 384)]
        sc[:, pl.ds(pl.multiple_of(t * 128, 128), 128)] = mm(window, pick).astype(BF16)

    store_branch = pltpu.make_async_copy(sc, branch_hbm, out_sem.at[8])
    store_branch.start()

    for copy in (s2[2], s2[3], r2[0], r2[1]):
        copy.wait_recv()

    def add_second(r):
        here = pl.ds(r, 16)
        summed[here, :] = (
            total[p2, here, :].astype(F32)
            + direct2[0, here, :].astype(F32)
            + direct2[1, here, :].astype(F32)
        ).astype(BF16)

    add_rows(PADDED, add_second)

    y_near = [
        remote(summed, ysum.at[0], ys.at[0], yr.at[0], at(x, y + 1, z, c)),
        remote(summed, ysum.at[1], ys.at[1], yr.at[1], at(x, y - 1, z, c)),
    ]
    y_far = remote(summed, ysum.at[2], ys.at[2], yr.at[2], at(x, y + 2, z, c))

    @pl.when(c != yl)
    def _():
        y_near[0].start()
        y_near[1].start()

    @pl.when(c == yl)
    def _():
        y_far.start()

    def backward(slot):
        owner = meta[2, slot]
        for h in range(HEADS):
            cols = slice(h * HEAD, (h + 1) * HEAD)
            kcols = slice(WIDTH + h * HEAD, WIDTH + (h + 1) * HEAD)
            vcols = slice(2 * WIDTH + h * HEAD, 2 * WIDTH + (h + 1) * HEAD)
            q, k, v = qkv[slot, :, cols], qkv[slot, :, kcols], qkv[slot, :, vcols]
            soft = soft_keep[owner, h]
            go = back_recv[owner, :, cols]
            out = att_send[owner, :, cols]
            delta = jnp.sum(go.astype(F32) * out.astype(F32), axis=-1, keepdims=True)
            gs = (soft * (mm(go, v, NT) - delta)).astype(BF16)
            qkv[slot, :, cols] = (mm(gs, k) * INV_SCALE).astype(BF16)
            qkv[slot, :, kcols] = (mm(gs, q, TN) * INV_SCALE).astype(BF16)
            qkv[slot, :, vcols] = mm(soft.astype(BF16), go, TN).astype(BF16)

    def store_slot(slot):
        return pltpu.make_async_copy(qkv.at[slot], qkv_grad_hbm.at[slot], out_sem.at[slot])

    for i in range(7):
        source = (d + 7 - i) % 8
        remote(back_send.at[source], back_recv.at[source], b2s.at[i], b2r.at[i], partner).wait_recv()

    @pl.loop(0, 4)
    def _(slot):
        backward(slot)
        store_slot(slot).start()

    keeper = x // 2
    f_block = x % 2
    f_copies = [
        remote(mixed, final.at[f_block], fs.at[n], fr.at[f_block], at(x + n, y, z, keeper))
        for n in range(4)
    ]

    @pl.when(c == yl)
    def _():
        for copy in (*y_near, y_far):
            copy.wait_recv()

        def add_y(r):
            here = pl.ds(r, 16)
            mixed[here, :] = (
                summed[here, :].astype(F32)
                + ysum[0, here, :].astype(F32)
                + ysum[1, here, :].astype(F32)
                + ysum[2, here, :].astype(F32)
            ).astype(BF16)

        add_rows(PADDED, add_y)
        for n in range(1, 4):
            f_copies[n].start()

        @pl.when(keeper != c)
        def _():
            f_copies[0].start()

    @pl.loop(4, IMGS)
    def _(slot):
        backward(slot)
        store_slot(slot).start()

    mine = (c == yl) & (keeper == c)
    for n in range(2):
        @pl.when(mine & (f_block == n))
        def _():
            final[n] = mixed[...]

        @pl.when(jnp.logical_not(mine & (f_block == n)))
        def _():
            remote(mixed, final.at[n], fs.at[0], fr.at[n], partner).wait_recv()

    @pl.loop(0, SHARD // 16)
    def _(r):
        here = pl.ds(pl.multiple_of(r * 16, 16), 16)
        wout[here, :BLOCK] = final[0, here, :].astype(F32)
        wout[here, SECOND:] = final[1, here, :].astype(F32)

    tail = SHARD - SHARD % 16
    wout[tail:, :BLOCK] = final[0, tail:, :].astype(F32)[: SHARD - tail]
    wout[tail:, SECOND:] = final[1, tail:, :].astype(F32)[: SHARD - tail]

    store_w = pltpu.make_async_copy(wout, weight_grad_hbm, out_sem.at[9])
    store_w.start()

    w_y.wait_send()

    @pl.when(c != yl)
    def _():
        w_c.wait_send()
        y_near[0].wait_send()
        y_near[1].wait_send()

    @pl.when(c == yl)
    def _():
        y_far.wait_send()
        for n in range(1, 4):
            f_copies[n].wait_send()

        @pl.when(keeper != c)
        def _():
            f_copies[0].wait_send()

    for i in range(7):
        att_copy(i).wait_send()
        back_copy(i).wait_send()
    for copy in (*w1, *w2, send_sx, send_aa, send_ga, send_bx, *s1, *r1, *s2, *r2):
        copy.wait_send()
    for slot in range(IMGS):
        store_slot(slot).wait()
    store_branch.wait()
    store_w.wait()


def per_device(
    qkv_rows, proj_weight, layer_scale, out_grad, patch_counts, loader_plan, row_offsets
):
    dp_index = lax.axis_index("dp")
    column = lax.axis_index("fsdp")
    col_plan = lax.dynamic_index_in_dim(loader_plan, column, 1, keepdims=False)
    col_counts = lax.dynamic_index_in_dim(patch_counts, column, 1, keepdims=False)
    my_plan = lax.dynamic_index_in_dim(col_plan, dp_index, 0, keepdims=False)
    my_counts = lax.dynamic_index_in_dim(col_counts, dp_index, 0, keepdims=False)
    my_offsets = row_offsets[dp_index, column]
    ids = jnp.arange(IMGS, dtype=jnp.int32)
    slot_pos = jnp.arange(MAXP, dtype=jnp.int32)
    slot_of_owner = (col_plan == dp_index).astype(jnp.int32)
    meta = jnp.stack(
        [
            jnp.sum(slot_of_owner * ids[None, :], axis=1),
            jnp.sum(slot_of_owner * col_counts, axis=1),
            jnp.sum(slot_of_owner * ids[:, None], axis=0),
        ]
    )
    image_of_loader = my_plan[None, :] == ids[:, None]
    offset_from = jnp.sum(jnp.where(image_of_loader, my_offsets[None, :], 0), axis=1)
    count_from = jnp.sum(jnp.where(image_of_loader, my_counts[None, :], 0), axis=1)
    source = jnp.where(
        slot_pos[None, :] < count_from[:, None], offset_from[:, None] + slot_pos[None, :], -1
    )
    scale_pad = jnp.pad(layer_scale.reshape(16, SHARD), ((0, 0), (0, PADDED - SHARD)))

    vmem = pl.BlockSpec(memory_space=pltpu.VMEM)
    hbm = pl.BlockSpec(memory_space=pl.ANY)
    dma = pltpu.SemaphoreType.DMA
    rows = (PADDED, BLOCK)
    branch, grads, weight_grad = pl.pallas_call(
        fused,
        out_shape=(
            jax.ShapeDtypeStruct((OWN, D), BF16),
            jax.ShapeDtypeStruct((IMGS, MAXP, 3 * WIDTH), BF16),
            jax.ShapeDtypeStruct((SHARD, WIDTH), F32),
        ),
        in_specs=[pl.BlockSpec(memory_space=pltpu.SMEM), hbm, hbm, hbm, vmem, vmem, vmem, vmem],
        out_specs=(hbm, hbm, hbm),
        scratch_shapes=[
            pltpu.VMEM((SHARD, WIDTH), BF16),
            pltpu.VMEM((PADDED, WIDTH), BF16),
            pltpu.VMEM((HALF, WIDTH), BF16),
            pltpu.VMEM((IMGS, MAXP, 3 * WIDTH), BF16),
            pltpu.VMEM((OWN, D), BF16),
            pltpu.VMEM((2 * OWN, HALF), BF16),
            pltpu.VMEM((OWN, HALF), BF16),
            pltpu.VMEM((IMGS, MAXP, WIDTH), BF16),
            pltpu.VMEM((IMGS, MAXP, WIDTH), BF16),
            pltpu.VMEM((2 * OWN, WIDTH), BF16),
            pltpu.VMEM((IMGS, HEADS, MAXP, MAXP), F32),
            pltpu.VMEM((2, HALF, BLOCK), BF16),
            pltpu.VMEM((2, 2, *rows), BF16),
            pltpu.VMEM((2, 4, *rows), BF16),
            pltpu.VMEM((4, *rows), BF16),
            pltpu.VMEM(rows, BF16),
            pltpu.VMEM((2, *rows), BF16),
            pltpu.VMEM(rows, BF16),
            pltpu.VMEM((3, *rows), BF16),
            pltpu.VMEM(rows, BF16),
            pltpu.VMEM((2, *rows), BF16),
            pltpu.VMEM((SHARD, WIDTH), F32),
            pltpu.VMEM((OWN, WIDTH), F32),
            pltpu.VMEM((OWN, WIDTH), F32),
            pltpu.VMEM((OWN, WIDTH), F32),
            pltpu.VMEM((IMGS, MAXP, WIDTH), BF16),
            pltpu.VMEM((IMGS, MAXP, WIDTH), BF16),
            pltpu.VMEM((OWN, 2 * HALF), BF16),
            pltpu.VMEM((OWN, HALF), BF16),
            dma((3,)),
            dma((2,)), dma((2,)),
            dma((6,)), dma((6,)),
            dma((7,)), dma((7,)),
            dma((4,)), dma((4,)),
            dma((12,)), dma((12,)),
            dma((6,)), dma((6,)),
            dma((3,)), dma((3,)),
            dma((4,)), dma((2,)),
            dma((7,)), dma((7,)),
            dma((10,)),
        ],
        compiler_params=pltpu.CompilerParams(
            collective_id=0, has_side_effects=True, vmem_limit_bytes=62 << 20
        ),
        cost_estimate=pl.CostEstimate(
            flops=13_000_000_000, bytes_accessed=20_000_000, transcendentals=500_000
        ),
        name="attention_sublayer",
    )(
        meta,
        proj_weight,
        qkv_rows[0, 0],
        out_grad[0, 0],
        layer_scale[None, :],
        scale_pad.reshape(1, 2 * HALF),
        source.reshape(1, IMGS * MAXP),
        source.reshape(IMGS * MAXP, 1),
    )
    return (branch[None, None], grads[None, None], weight_grad)


def solution(mesh):
    in_specs = (
        P("dp", "fsdp", None, None, None),
        P("fsdp", None),
        P(),
        P("dp", "fsdp", None, None),
        P(),
        P(),
        P(),
    )
    out_specs = (P("dp", "fsdp", None, None), P("dp", "fsdp", None, None, None), P("fsdp", None))
    return jax.shard_map(
        per_device, mesh=mesh, in_specs=in_specs, out_specs=out_specs, check_vma=False
    )
```

time: 360 us -> 187 us (0.52)
  Pallas kernels: 0 us -> 168 us
  waiting for transfers between devices: 130 us -> 0 us
  blocking collectives: 116 us -> 0 us
  matrix products: 51 us -> 0 us
  local copies, waits for them, and re-layouts: 32.7 us -> 16.6 us
  between operations: 14.2 us -> 0.68 us
  other arithmetic: 8.8 us -> 1 us
  starting transfers between devices: 6.96 us -> 0 us
    pallas_call x0 -> x1, Pallas kernels: none -> 168 us  [per_device(): pl.pallas_call(fused, out_shape=(jax.ShapeDtypeStruct((OWN, D), BF16), ja...]
    psum x1 -> x0, blocking collectives: 88.9 us -> none  [per_device(): weight_grad = lax.psum(shard_sum.astype(jnp.float32), 'dp')]
    all_gather x1 -> x0, waiting for transfers between devices: 63.8 us -> none  [per_device(): weights = lax.all_gather(proj_weight, 'fsdp', axis=0, tiled=True)]
    dot_general x12 -> x0, matrix products: 51 us -> none  [the longest x1 11.5 us: project(): lax.dot_general(attended, weights, (((1,), (1,)), ((), ())), preferred_el...]
    unnamed x3 -> x0, waiting for transfers between devices: 49.5 us -> none
    all_to_all x1 -> x0, blocking collectives: 26.6 us -> none  [per_device(): lax.all_to_all(outgoing.reshape(dp_count, slot_len, width), 'dp', split_a...]
    all_to_all x1 -> x0, waiting for transfers between devices: 16.6 us -> none  [per_device(): lax.all_to_all(back_send.reshape(dp_count, slot_len, width), 'dp', split_...]
    concatenate x3 -> x0, local copies, waits for them, and re-layouts: 10.6 us -> none  [attend_back(): jnp.concatenate([grad_query.reshape(shape_lead + (width_all,)), grad_key....]
  transfers between devices with their start and end apart: 3 -> 0, of which waited for: 3 -> 0; matrix products, arithmetic and copies ran while one was open for 15% -> 0% of each run, Pallas kernels for 0% -> 0%
where the time goes in v2:
time: 187 us; the launch traced here: 186 us
  Pallas kernels  168 us (90%)
  local copies, waits for them, and re-layouts  16.6 us (9%)
    pallas_call x1, Pallas kernels, per_device(): pl.pallas_call(fused, out_shape=(jax.ShapeDtypeStruct((OWN, D), BF16), ja...  168 us
    unnamed x9, local copies, waits for them, and re-layouts  10.3 us

profile of v2, /device:TPU:0, one launch (start us, length us, event | category | flops | bytes accessed | tf_op | source)
XLA Modules:
  0.0 186.3 jit_solution(3526791861461025599)
XLA Ops:
  0.6 0.0 copy-start
  0.7 0.7 copy-done
  1.4 0.2 dynamic-slice_reduce_fusion
  1.6 0.9 dynamic-slice_reduce_fusion.1
  2.5 0.2 select_reduce_fusion.1
  2.7 0.1 add_select_fusion
  2.7 0.7 select_n.54.source_row
  3.4 1.3 broadcast_in_dim.42.scale
  4.7 0.8 reshape.121
  5.5 0.7 reshape.122.scale_pad
  6.2 0.8 constant_dynamic-slice_fusion
  7.1 0.1 copy.16
  7.2 0.1 copy.15
  7.3 0.2 select_reduce_fusion.3
  7.5 0.6 pad_add_fusion.meta
  8.1 0.9 select_n.56.source_col
  9.0 168.0 %attention_sublayer.1 = (bf16[320,3200]{1,0:T(8,128)(2,1)}, bf16[8,64,4992]{2,1,0:T(8,128)(2,1)}, f32[200,1664]{1,0:T(8,128)}) custom-call(s32[3,8]{1,0:T(4,128)} %pad_add_fusion.meta, bf16[200,1664]{1,0:T(8,128)(2,1)} %shard_hbm.1, bf16[8,64,4992]{2,1,0:T(8,128)(2,1)} %bitcast.20, bf16[320,3200]{1,0:T(8,128)(2,1)} %bitcast.21, ...), custom_call_target="tpu_custom_call" | custom-call | flops 12999999488 | bytes 20000000 | tf_op jit(solution)/shard_map/attention_sublayer/pallas_call | solution.py:567
  177.0 3.0 %copy.20 = bf16[1,1,320,3200]{3,2,1,0:T(8,128)(2,1)} copy(bf16[1,1,320,3200]{3,2,1,0:T(8,128)(2,1)} %bitcast.16) | data formatting | bytes 4096000
  180.0 0.0 copy-start.1
  180.0 5.2 %copy.21 = bf16[1,1,8,64,4992]{4,3,2,1,0:T(8,128)(2,1)} copy(bf16[1,1,8,64,4992]{4,3,2,1,0:T(8,128)(2,1)} %bitcast.15) | data formatting | bytes 10223616
  185.3 0.0 copy-done.1
  185.3 1.1 copy.22
  (1 shorter events, 0.0 us)
Async XLA Ops:
  0.6 0.8 copy-start
  180.0 5.2 %copy-start.1 = (f32[200,1664]{1,0:T(8,128)S(1)}, f32[200,1664]{1,0:T(8,128)}, u32[]{:S(2)}) copy-start(f32[200,1664]{1,0:T(8,128)} %get-tuple-element.23) | copy-start | bytes 3993604

commit v3 on v2

v3 whole, which is shorter than its diff:
```python
import math

import jax
import jax.numpy as jnp
from jax import lax
from jax.experimental import pallas as pl
from jax.experimental.pallas import tpu as pltpu
from jax.sharding import PartitionSpec as P

HEADS = 13
HEAD = 128
WIDTH = HEADS * HEAD
D = 3200
IMGS = 8
MAXP = 64
OWN = 320
SHARD = 200
PADDED = 208
HALF = 8 * PADDED
BLOCK = 896
SECOND = WIDTH - BLOCK
CUT = 96
MASKED = -1e30
TURNS = 0o06725341
MESH = pl.DeviceIdType.MESH
INV_SCALE = 1.0 / math.sqrt(HEAD)
F32 = jnp.float32
BF16 = jnp.bfloat16

NN = (((1,), (0,)), ((), ()))
NT = (((1,), (1,)), ((), ()))
TN = (((0,), (0,)), ((), ()))


def mm(a, b, dims=NN):
    return lax.dot_general(a, b, dims, preferred_element_type=F32)


def two_heads(rows):
    none = jnp.zeros((MAXP, HEAD), BF16)
    upper = jnp.concatenate([rows[:, :HEAD], none], axis=1)
    lower = jnp.concatenate([none, rows[:, HEAD:]], axis=1)
    return jnp.concatenate([upper, lower], axis=0)


def stacked(rows):
    return two_heads(rows) if rows.shape[1] > HEAD else rows


def side_by_side(product):
    if product.shape[0] == MAXP:
        return product
    return jnp.concatenate([product[:MAXP, :HEAD], product[MAXP:, HEAD:]], axis=1)


def unit_columns(unit):
    return slice(2 * unit * HEAD, min(2 * unit + 2, HEADS) * HEAD)


def by_columns(body):
    @pl.loop(0, WIDTH // 256)
    def _(n):
        body(pl.multiple_of(n * 256, 128), 256)

    body(WIDTH - WIDTH % 256, WIDTH % 256)


def spread_tile(tile):
    first = tile * 128
    group = first // PADDED
    inside = first % PADDED
    start = lax.min((group * SHARD + lax.min(inside, SHARD)) // 128, D // 128 - 2)
    place = first + lax.broadcasted_iota(jnp.int32, (256, 128), 1)
    source = start * 128 + lax.broadcasted_iota(jnp.int32, (256, 128), 0)
    groups = group + (place >= (group + 1) * PADDED).astype(jnp.int32)
    local = place - groups * PADDED
    hit = (source == groups * SHARD + local) & (local < SHARD)
    return start * 128, jnp.where(hit, 1.0, 0.0).astype(BF16)


def compact_tile(tile):
    first = tile * 128
    group = first // SHARD
    start = lax.min((first + group * (PADDED - SHARD)) // 128, 2 * HALF // 128 - 3)
    place = first + lax.broadcasted_iota(jnp.int32, (384, 128), 1)
    source = start * 128 + lax.broadcasted_iota(jnp.int32, (384, 128), 0)
    groups = group + (place >= (group + 1) * SHARD).astype(jnp.int32)
    hit = source == place + groups * (PADDED - SHARD)
    return start * 128, jnp.where(hit, 1.0, 0.0).astype(BF16)


def fused(
    tables, shard_hbm, qkv_hbm, grad_hbm, scale,
    branch_hbm, qkv_grad_hbm, final_hbm,
    meta, wv, wp, wh, qkv, sc, scale_parts, scale_pad, sp, sx, att_send, att_recv, aa, soft_keep,
    gh, relay, direct, total, relay2, direct2, summed, ysum, mixed, final,
    ga_own, ga_send, ga_recv, back_send, back_recv, bx,
    in_sem, w0s, w0r, w1s, w1r, a2s, a2r, cs, cr, g1s, g1r, g2s, g2r, ys, yr, fs, fr, b2s, b2r, out_sem,
):
    d = lax.axis_index("dp")
    f = lax.axis_index("fsdp")
    c = f % 2
    z = (f // 2) % 4
    yl = f // 8
    x = d // 2
    y = (d % 2) * 2 + yl

    def at(px, py, pz, pc):
        px, py, pz = (px + 4) % 4, (py + 4) % 4, (pz + 4) % 4
        return (px * 2 + py // 2, ((py % 2) * 4 + pz) * 2 + pc)

    def remote(src, dst, send, recv, dev):
        return pltpu.make_async_remote_copy(
            src_ref=src, dst_ref=dst, send_sem=send, recv_sem=recv, device_id=dev, device_id_type=MESH
        )

    partner = at(x, y, z, 1 - c)

    load_w = pltpu.make_async_copy(shard_hbm, wv, in_sem.at[0])
    load_q = pltpu.make_async_copy(qkv_hbm, qkv, in_sem.at[1])
    load_g = pltpu.make_async_copy(grad_hbm, sc, in_sem.at[2])
    load_w.start()
    load_q.start()
    load_g.start()

    barrier = pltpu.get_barrier_semaphore()
    peers = []
    for step in range(1, 8):
        other = (d + step) % 8
        peers += [(other, f), (other, f + 1 - 2 * c)]
    peers += [partner, at(x, y, z + 1, c), at(x, y, z - 1, c)]
    for sign in (1, -1):
        peers += [at(x, y + sign, z, 0), at(x, y + sign, z, 1)]
    for peer in peers:
        pl.semaphore_signal(barrier, inc=1, device_id=peer, device_id_type=MESH)
    owner_of = [(d + 8 - tables[0, 0, k]) % 8 for k in range(IMGS)]
    for k in range(IMGS):
        meta[2, k] = owner_of[k]
    image_offset, image_count = [], []
    for e in range(8):
        slot, image = 0, 0
        for k in range(1, IMGS):
            slot = jnp.where(owner_of[k] == e, k, slot)
            image = jnp.where(tables[0, d, k] == e, k, image)
        meta[0, e] = slot
        meta[1, e] = tables[1, e, slot]
        image_offset.append(tables[2, d, image])
        image_count.append(tables[1, d, image])
    load_w.wait()
    wp[0:192, :] = wv[0:192, :]
    wp[192:208, :] = jnp.concatenate(
        [wv[192:200, :].astype(F32), jnp.zeros((8, WIDTH), F32)], axis=0
    ).astype(BF16)
    pl.semaphore_wait(barrier, len(peers))

    def w_rows(pz, k):
        return wh.at[pl.ds(pl.multiple_of((((pz + 4) % 4) * 2 + k) * PADDED, 16), PADDED), :]

    w_y = remote(wp, w_rows(z, c), w0s.at[0], w0r.at[c], at(x, y + 1 - 2 * c, z, yl))
    w_c = remote(wp, w_rows(z, c), w0s.at[1], w0r.at[c], partner)
    w_l = pltpu.make_async_copy(wp, w_rows(z, c), w0s.at[1])
    w_y.start()

    @pl.when(c == yl)
    def _():
        w_l.start()

    @pl.when(c != yl)
    def _():
        w_c.start()

    load_q.wait()

    def partner_at(i, sign=1):
        n = TURNS // 8**i % 8 if isinstance(i, int) else lax.div(TURNS, lax.shift_left(1, 3 * i)) % 8
        return ((x + sign * (n % 4) + 4) % 4) * 2 + (d + n // 4) % 2

    def att_copy(i):
        owner = partner_at(i)
        return remote(att_send.at[owner], att_recv.at[d], a2s.at[i], a2r.at[i], (owner, f))

    @pl.loop(0, IMGS)
    def _(i):
        owner = partner_at(i)
        slot = meta[0, owner]
        count = meta[1, owner]
        for units in ((0, 1, 2, 3), (4, 5, 6)):
            scores = []
            for u in units:
                cols = unit_columns(u)
                q = qkv[slot, :, cols]
                k = qkv[slot, :, WIDTH + cols.start : WIDTH + cols.stop]
                scores.append(mm(k, stacked(q), NT) * INV_SCALE)
            softs = []
            for u, s in zip(units, scores):
                s = jnp.where(lax.broadcasted_iota(jnp.int32, s.shape, 0) < count, s, MASKED)
                e = jnp.exp(s - jnp.max(s, axis=0, keepdims=True))
                soft = e * (1.0 / jnp.sum(e, axis=0, keepdims=True))
                soft_keep[owner, u, :, : s.shape[1]] = soft
                softs.append(soft.astype(BF16))
            for u, soft in zip(units, softs):
                cols = unit_columns(u)
                v = qkv[slot, :, 2 * WIDTH + cols.start : 2 * WIDTH + cols.stop]
                att_send[owner, :, cols] = side_by_side(mm(soft, v, TN)).astype(BF16)

        @pl.when(i < 7)
        def _():
            att_copy(i).start()

    att_recv[d] = att_send[d]

    for k in range(2):
        @pl.when((c != yl) | (c != k))
        def _():
            remote(wp, w_rows(z, k), w0s.at[0], w0r.at[k], partner).wait_recv()

    @pl.when(c == yl)
    def _():
        w_l.wait()

    up, down = at(x, y, z + 1, c), at(x, y, z - 1, c)
    w1 = [
        remote(w_rows(z, 0), w_rows(z, 0), w1s.at[0], w1r.at[0], up),
        remote(w_rows(z, 1), w_rows(z, 1), w1s.at[1], w1r.at[1], down),
        remote(w_rows(z, 1), w_rows(z, 1), w1s.at[2], w1r.at[2], up),
        remote(w_rows(z, 0), w_rows(z, 0), w1s.at[3], w1r.at[3], down),
    ]
    for copy in w1:
        copy.start()
    w2 = [
        remote(w_rows(z - 1, 0), w_rows(z - 1, 0), w1s.at[4], w1r.at[4], up),
        remote(w_rows(z + 1, 1), w_rows(z + 1, 1), w1s.at[5], w1r.at[5], down),
    ]

    load_g.wait()

    scale_row = scale[...].reshape(1, D)

    @pl.loop(0, OWN // 16)
    def _(r):
        rows = pl.ds(pl.multiple_of(r * 16, 16), 16)
        sc[rows, :] = (sc[rows, :].astype(F32) * scale_row).astype(BF16)

    high_part = scale_row.astype(BF16).astype(F32)
    mid_part = (scale_row - high_part).astype(BF16).astype(F32)
    low_part = scale_row - high_part - mid_part
    part = lax.broadcasted_iota(jnp.int32, (16, D), 0)
    scale_parts[...] = jnp.where(
        part == 0, high_part, jnp.where(part == 1, mid_part, jnp.where(part == 2, low_part, 0.0))
    ).astype(BF16)

    own_rows = pl.ds(pl.multiple_of(c * OWN, 16), OWN)
    other_rows = pl.ds(pl.multiple_of((1 - c) * OWN, 16), OWN)

    @pl.loop(0, HALF // 128, unroll=True)
    def _(t):
        start, pick = spread_tile((1 - c) * (HALF // 128) + t)
        window = sc[:, pl.ds(pl.multiple_of(start, 128), 256)]
        sx[:, pl.ds(pl.multiple_of(t * 128, 128), 128)] = mm(window, pick).astype(BF16)

    send_sx = remote(sx, sp.at[own_rows, :], cs.at[0], cr.at[0], partner)
    send_sx.start()

    @pl.loop(0, HALF // 128, unroll=True)
    def _(t):
        start, pick = spread_tile(c * (HALF // 128) + t)
        window = sc[:, pl.ds(pl.multiple_of(start, 128), 256)]
        there = pl.ds(pl.multiple_of(t * 128, 128), 128)
        sp[own_rows, there] = mm(window, pick).astype(BF16)
        parts = mm(scale_parts[:, pl.ds(pl.multiple_of(start, 128), 256)], pick)
        scale_pad[:, there] = jnp.sum(parts, axis=0, keepdims=True)

    w1[0].wait_recv()
    w2[0].start()
    w1[1].wait_recv()
    w2[1].start()

    for i in range(7):
        source = partner_at(i, -1)
        remote(att_send.at[source], att_recv.at[source], a2s.at[i], a2r.at[i], partner).wait_recv()
    lane = lax.broadcasted_iota(jnp.int32, (1, IMGS * MAXP), 1)
    source_row = jnp.full((1, IMGS * MAXP), -1, jnp.int32)
    for n in range(8):
        inside = lane - n * MAXP
        source_row = jnp.where(
            (inside >= 0) & (inside < image_count[n]), inside + image_offset[n], source_row
        )
    pack = jnp.where(
        lax.broadcasted_iota(jnp.int32, (OWN, IMGS * MAXP), 0) == source_row, 1.0, 0.0
    ).astype(BF16)

    def pack_columns(start, size):
        got = att_recv[:, :, pl.ds(start, size)].reshape(IMGS * MAXP, size)
        aa[own_rows, pl.ds(start, size)] = mm(pack, got).astype(BF16)

    by_columns(pack_columns)
    send_aa = remote(aa.at[own_rows, :], aa.at[own_rows, :], cs.at[1], cr.at[1], partner)
    send_aa.start()
    remote(sx, sp.at[other_rows, :], cs.at[0], cr.at[0], partner).wait_recv()
    remote(aa.at[other_rows, :], aa.at[other_rows, :], cs.at[1], cr.at[1], partner).wait_recv()

    def block(first, second):
        first, second = (first + 4) % 4, (second + 4) % 4
        return first % 2, pl.ds(pl.multiple_of((second * 2 + first // 2) * PADDED, 16), PADDED)

    p1 = y * (1 - c) + x * c
    p2 = z
    right1, left1 = at(x + c, y + 1 - c, z, c), at(x - c, y - 1 + c, z, c)
    right2, left2 = up, down

    def g1(first, j, dst, sem, dev):
        h, rows = block(first, j)
        return remote(gh.at[h, rows, :], dst, g1s.at[sem], g1r.at[sem], dev)

    s1 = [g1(p1 + 2, j, relay.at[0, j], j, right1) for j in (0, 1)]
    s1 += [g1(p1 + 2, j, relay.at[1, j - 2], j, left1) for j in (2, 3)]
    s1 += [g1(p1 + 1, j, direct.at[0, j], 4 + j, right1) for j in (2, 3)]
    s1 += [g1(p1 - 1, j, direct.at[1, j], 8 + j, left1) for j in (0, 1)]

    def weight_columns(h):
        cols = pl.ds(pl.multiple_of(h * SECOND, 128), BLOCK)

        @pl.loop(0, HALF // 128)
        def _(t):
            rows = pl.ds(pl.multiple_of(t * 128, 128), 128)
            gh[h, rows, :] = mm(sp[:, rows], aa[:, cols], TN).astype(BF16)

    weight_columns(p1 % 2)
    for copy in (s1[0], s1[2], s1[1], s1[3]):
        copy.start()
    weight_columns(1 - p1 % 2)
    for copy in (s1[4], s1[6], s1[5], s1[7]):
        copy.start()
    r1 = [g1(p1 + 1, j, direct.at[0, j], 4 + j, right1) for j in (0, 1)]
    r1 += [g1(p1 - 1, j, direct.at[1, j], 8 + j, left1) for j in (2, 3)]

    def add_rows(rows, body):
        @pl.loop(0, rows // 16)
        def _(r):
            body(pl.multiple_of(r * 16, 16))

    for n, j in enumerate((0, 2, 1, 3)):
        side, place = (0, p1 + 1) if j < 2 else (1, p1 - 1)
        s1[j].wait_recv()
        h, rows = block(place, j)
        base = rows.start

        def add_relay(r, h=h, base=base, side=side, j=j):
            here = pl.ds(pl.multiple_of(base + r, 16), 16)
            gh[h, here, :] = (
                gh[h, here, :].astype(F32) + relay[side, j % 2, pl.ds(r, 16), :].astype(F32)
            ).astype(BF16)

        add_rows(PADDED, add_relay)
        r1[j].start()

    w1[2].wait_recv()
    w1[3].wait_recv()
    w2[0].wait_recv()
    w2[1].wait_recv()

    def grad_columns(start, size):
        cols = pl.ds(start, size)
        ga_send[:, cols] = mm(sp[other_rows, :], wh[:, cols])
        ga_own[:, cols] = mm(sp[own_rows, :], wh[:, cols])

    by_columns(grad_columns)
    send_ga = remote(ga_send, ga_recv, cs.at[2], cr.at[2], partner)
    send_ga.start()
    send_ga.wait_recv()
    unpack = []
    for n in range(8):
        inside = lax.broadcasted_iota(jnp.int32, (MAXP, OWN), 0)
        column = lax.broadcasted_iota(jnp.int32, (MAXP, OWN), 1)
        hit = (inside < image_count[n]) & (column == inside + image_offset[n])
        unpack.append(jnp.where(hit, 1.0, 0.0).astype(BF16))
    unpack = jnp.concatenate(unpack, axis=0)

    def unpack_columns(start, size):
        cols = pl.ds(start, size)
        grad = (ga_own[:, cols] + ga_recv[:, cols]).astype(BF16)
        back_send[:, :, cols] = mm(unpack, grad).astype(BF16).reshape(IMGS, MAXP, size)

    by_columns(unpack_columns)

    def back_copy(i):
        loader = partner_at(i)
        return remote(back_send.at[loader], back_recv.at[d], b2s.at[i], b2r.at[i], (loader, f))

    for i in range(7):
        back_copy(i).start()
    back_recv[d] = back_send[d]

    for j in range(4):
        (s1[4 + j - 2] if j >= 2 else r1[j]).wait_recv()
        (s1[6 + j] if j < 2 else r1[j]).wait_recv()
        h, rows = block(p1, j)
        base = rows.start

        def add_first(r, h=h, base=base, j=j):
            here = pl.ds(r, 16)
            total[j, here, :] = (
                gh[h, pl.ds(pl.multiple_of(base + r, 16), 16), :].astype(F32)
                + direct[0, j, here, :].astype(F32)
                + direct[1, j, here, :].astype(F32)
            ).astype(BF16)

        add_rows(PADDED, add_first)

    low, high = pl.ds(0, CUT), pl.ds(CUT, PADDED - CUT)

    def g2(place, rows, dst, sem, dev):
        return remote(total.at[(place + 4) % 4, rows, :], dst, g2s.at[sem], g2r.at[sem], dev)

    s2 = [
        g2(p2 + 2, low, relay2.at[low, :], 0, right2),
        g2(p2 + 2, high, relay2.at[high, :], 1, left2),
        g2(p2 + 1, high, direct2.at[0, high, :], 2, right2),
        g2(p2 - 1, low, direct2.at[1, low, :], 3, left2),
    ]
    r2 = [
        g2(p2 + 1, low, direct2.at[0, low, :], 4, right2),
        g2(p2 - 1, high, direct2.at[1, high, :], 5, left2),
    ]
    for copy in s2:
        copy.start()

    def project_rows(start, size):
        cols = pl.ds(start, size)
        bx[:, cols] = (scale_pad[:, cols] * mm(aa[...], wh[cols, :], NT)).astype(BF16)

    by_columns(project_rows)
    my_half = branch_hbm.at[:, pl.ds(pl.multiple_of(c * HALF, 128), HALF)]
    other_half = branch_hbm.at[:, pl.ds(pl.multiple_of((1 - c) * HALF, 128), HALF)]
    send_bx = remote(bx.at[other_rows, :], my_half, cs.at[3], cr.at[3], partner)
    send_bx.start()
    store_branch = pltpu.make_async_copy(bx.at[own_rows, :], my_half, out_sem.at[8])
    store_branch.start()

    for side in range(2):
        s2[side].wait_recv()
        place = (p2 + 1 if side == 0 else p2 + 3) % 4
        offset, rows = (0, CUT) if side == 0 else (CUT, PADDED - CUT)

        def add_relay2(r, place=place, offset=offset):
            here = pl.ds(pl.multiple_of(offset + r, 16), 16)
            total[place, here, :] = (
                total[place, here, :].astype(F32) + relay2[here, :].astype(F32)
            ).astype(BF16)

        add_rows(rows, add_relay2)
        r2[side].start()

    for copy in (s2[2], s2[3], r2[0], r2[1]):
        copy.wait_recv()

    def add_second(r):
        here = pl.ds(r, 16)
        summed[here, :] = (
            total[p2, here, :].astype(F32)
            + direct2[0, here, :].astype(F32)
            + direct2[1, here, :].astype(F32)
        ).astype(BF16)

    add_rows(PADDED, add_second)

    s3 = [
        remote(summed, ysum.at[n], ys.at[n], yr.at[n], at(x + (1 - c) * m, y + c * m, z, c))
        for n, m in enumerate((1, 3, 2))
    ]
    for copy in s3:
        copy.start()

    def backward(slot):
        owner = meta[2, slot]
        for units in ((0, 1, 2), (3, 4), (5, 6)):
            stages = []
            for u in units:
                cols = unit_columns(u)
                v = qkv[slot, :, 2 * WIDTH + cols.start : 2 * WIDTH + cols.stop]
                go = stacked(back_recv[owner, :, cols])
                soft = soft_keep[owner, u, :, : go.shape[0]]
                stages.append((u, go, soft, mm(v, go, NT)))
            for u, go, soft, grad_soft in stages:
                cols = unit_columns(u)
                kcols = slice(WIDTH + cols.start, WIDTH + cols.stop)
                vcols = slice(2 * WIDTH + cols.start, 2 * WIDTH + cols.stop)
                q, k = stacked(qkv[slot, :, cols]), qkv[slot, :, kcols]
                delta = jnp.sum(soft * grad_soft, axis=0, keepdims=True)
                gs = (soft * (grad_soft - delta)).astype(BF16)
                grad_v = mm(soft.astype(BF16), go)
                grad_k = mm(gs, q) * INV_SCALE
                grad_q = side_by_side(mm(gs, k, TN)) * INV_SCALE
                qkv[slot, :, vcols] = grad_v.astype(BF16)
                qkv[slot, :, kcols] = grad_k.astype(BF16)
                qkv[slot, :, cols] = grad_q.astype(BF16)

    def store_slot(slot):
        return pltpu.make_async_copy(qkv.at[slot], qkv_grad_hbm.at[slot], out_sem.at[slot])

    for copy in s3:
        copy.wait_recv()

    def add_third(r):
        here = pl.ds(r, 16)
        mixed[here, :] = (
            summed[here, :].astype(F32)
            + ysum[0, here, :].astype(F32)
            + ysum[1, here, :].astype(F32)
            + ysum[2, here, :].astype(F32)
        ).astype(BF16)

    add_rows(PADDED, add_third)
    keeper = p1 // 2
    column = p1 % 2
    mine = (c == yl) & (keeper == c)

    def f_copy(n, dev):
        return remote(mixed, final.at[column], fs.at[n], fr.at[column], dev)

    f_y = [f_copy(n, at(x, 2 * n, z, keeper)) for n in range(2)]
    f_x = [f_copy(n, at(x + n, y, z, keeper)) for n in range(4)]

    def for_spread(act):
        for n in range(2):
            @pl.when((c == 0) & jnp.logical_not(mine & (y == 2 * n)))
            def _():
                act(f_y[n])

        @pl.when((c == 1) & (yl == 1))
        def _():
            for n in (1, 3, 2):
                act(f_x[n])

            @pl.when(jnp.logical_not(mine))
            def _():
                act(f_x[0])

    for_spread(lambda copy: copy.start())

    for i in range(7):
        source = partner_at(i, -1)
        remote(back_send.at[source], back_recv.at[source], b2s.at[i], b2r.at[i], partner).wait_recv()

    @pl.loop(0, IMGS)
    def _(slot):
        backward(slot)
        store_slot(slot).start()

    for n in range(2):
        @pl.when(mine & (column == n))
        def _():
            final[n] = mixed[...]

        @pl.when(jnp.logical_not(mine & (column == n)))
        def _():
            remote(mixed, final.at[n], fs.at[0], fr.at[n], partner).wait_recv()

    store_w = pltpu.make_async_copy(final, final_hbm, out_sem.at[9])
    store_w.start()
    send_bx_recv = remote(bx.at[other_rows, :], other_half, cs.at[3], cr.at[3], partner)
    send_bx_recv.wait_recv()

    w_y.wait_send()

    @pl.when(c != yl)
    def _():
        w_c.wait_send()

    for_spread(lambda copy: copy.wait_send())
    for i in range(7):
        att_copy(i).wait_send()
        back_copy(i).wait_send()
    for copy in (*w1, *w2, send_sx, send_aa, send_ga, send_bx, *s1, *r1, *s2, *r2, *s3):
        copy.wait_send()
    for slot in range(IMGS):
        store_slot(slot).wait()
    store_branch.wait()
    store_w.wait()


def finish(
    branch_hbm, grads_hbm, sums_hbm, branch_out, grads_out, weight_out,
    padded, grads, sums, branch, weight, in_sem, out_sem,
):
    load_branch = pltpu.make_async_copy(branch_hbm, padded, in_sem.at[8])
    load_sums = pltpu.make_async_copy(sums_hbm, sums, in_sem.at[9])
    loads = [pltpu.make_async_copy(grads_hbm.at[k], grads.at[k], in_sem.at[k]) for k in range(IMGS)]
    stores = [pltpu.make_async_copy(grads.at[k], grads_out.at[k], out_sem.at[k]) for k in range(IMGS)]
    store_branch = pltpu.make_async_copy(branch, branch_out, out_sem.at[8])
    store_weight = pltpu.make_async_copy(weight, weight_out, out_sem.at[9])
    load_branch.start()
    load_sums.start()
    for load in loads:
        load.start()
    load_sums.wait()
    weight[:, :BLOCK] = sums[0].astype(F32)[:SHARD]
    weight[:, SECOND:] = sums[1].astype(F32)[:SHARD]
    store_weight.start()
    load_branch.wait()
    for k in range(IMGS):
        loads[k].wait()
        stores[k].start()

    @pl.loop(0, D // 128, unroll=5)
    def _(t):
        start, pick = compact_tile(t)
        window = padded[:, pl.ds(pl.multiple_of(start, 128), 384)]
        branch[:, pl.ds(pl.multiple_of(t * 128, 128), 128)] = mm(window, pick).astype(BF16)

    store_branch.start()
    for store in (store_weight, *stores, store_branch):
        store.wait()


def per_device(
    qkv_rows, proj_weight, layer_scale, out_grad, patch_counts, loader_plan, row_offsets
):
    tables = jnp.stack([loader_plan, patch_counts, row_offsets])
    tables = lax.dynamic_index_in_dim(tables, lax.axis_index("fsdp"), 2, keepdims=False)
    vmem = pl.BlockSpec(memory_space=pltpu.VMEM)
    smem = pl.BlockSpec(memory_space=pltpu.SMEM)
    hbm = pl.BlockSpec(memory_space=pl.ANY)
    dma = pltpu.SemaphoreType.DMA
    rows = (PADDED, BLOCK)
    grads_shape = jax.ShapeDtypeStruct((IMGS, MAXP, 3 * WIDTH), BF16)
    padded_branch, grads, sums = pl.pallas_call(
        fused,
        out_shape=(
            jax.ShapeDtypeStruct((OWN, 2 * HALF), BF16),
            grads_shape,
            jax.ShapeDtypeStruct((2, *rows), BF16),
        ),
        in_specs=[smem, hbm, hbm, hbm, vmem],
        out_specs=(hbm, hbm, hbm),
        scratch_shapes=[
            pltpu.SMEM((3, 8), jnp.int32),
            pltpu.VMEM((SHARD, WIDTH), BF16),
            pltpu.VMEM((PADDED, WIDTH), BF16),
            pltpu.VMEM((HALF, WIDTH), BF16),
            pltpu.VMEM((IMGS, MAXP, 3 * WIDTH), BF16),
            pltpu.VMEM((OWN, D), BF16),
            pltpu.VMEM((16, D), BF16),
            pltpu.VMEM((1, HALF), F32),
            pltpu.VMEM((2 * OWN, HALF), BF16),
            pltpu.VMEM((OWN, HALF), BF16),
            pltpu.VMEM((IMGS, MAXP, WIDTH), BF16),
            pltpu.VMEM((IMGS, MAXP, WIDTH), BF16),
            pltpu.VMEM((2 * OWN, WIDTH), BF16),
            pltpu.VMEM((IMGS, (HEADS + 1) // 2, MAXP, 2 * MAXP), F32),
            pltpu.VMEM((2, HALF, BLOCK), BF16),
            pltpu.VMEM((2, 2, *rows), BF16),
            pltpu.VMEM((2, 4, *rows), BF16),
            pltpu.VMEM((4, *rows), BF16),
            pltpu.VMEM(rows, BF16),
            pltpu.VMEM((2, *rows), BF16),
            pltpu.VMEM(rows, BF16),
            pltpu.VMEM((3, *rows), BF16),
            pltpu.VMEM(rows, BF16),
            pltpu.VMEM((2, *rows), BF16),
            pltpu.VMEM((OWN, WIDTH), F32),
            pltpu.VMEM((OWN, WIDTH), F32),
            pltpu.VMEM((OWN, WIDTH), F32),
            pltpu.VMEM((IMGS, MAXP, WIDTH), BF16),
            pltpu.VMEM((IMGS, MAXP, WIDTH), BF16),
            pltpu.VMEM((2 * OWN, HALF), BF16),
            dma((3,)),
            dma((2,)), dma((2,)),
            dma((6,)), dma((6,)),
            dma((7,)), dma((7,)),
            dma((4,)), dma((4,)),
            dma((12,)), dma((12,)),
            dma((6,)), dma((6,)),
            dma((3,)), dma((3,)),
            dma((4,)), dma((2,)),
            dma((7,)), dma((7,)),
            dma((10,)),
        ],
        compiler_params=pltpu.CompilerParams(
            collective_id=0, has_side_effects=True, vmem_limit_bytes=62 << 20
        ),
        cost_estimate=pl.CostEstimate(
            flops=13_000_000_000, bytes_accessed=20_000_000, transcendentals=500_000
        ),
        name="attention_sublayer",
    )(
        tables,
        proj_weight,
        qkv_rows[0, 0],
        out_grad[0, 0],
        layer_scale,
    )
    branch, grads, weight_grad = pl.pallas_call(
        finish,
        out_shape=(
            jax.ShapeDtypeStruct((OWN, D), BF16),
            grads_shape,
            jax.ShapeDtypeStruct((SHARD, WIDTH), F32),
        ),
        in_specs=[hbm, hbm, hbm],
        out_specs=(hbm, hbm, hbm),
        scratch_shapes=[
            pltpu.VMEM((OWN, 2 * HALF), BF16),
            pltpu.VMEM((IMGS, MAXP, 3 * WIDTH), BF16),
            pltpu.VMEM((2, *rows), BF16),
            pltpu.VMEM((OWN, D), BF16),
            pltpu.VMEM((SHARD, WIDTH), F32),
            dma((10,)),
            dma((10,)),
        ],
        compiler_params=pltpu.CompilerParams(vmem_limit_bytes=60 << 20),
        name="finish",
    )(padded_branch, grads, sums)
    return (branch[None, None], grads[None, None], weight_grad)


def solution(mesh):
    in_specs = (
        P("dp", "fsdp", None, None, None),
        P("fsdp", None),
        P(),
        P("dp", "fsdp", None, None),
        P(),
        P(),
        P(),
    )
    out_specs = (P("dp", "fsdp", None, None), P("dp", "fsdp", None, None, None), P("fsdp", None))
    return jax.shard_map(
        per_device, mesh=mesh, in_specs=in_specs, out_specs=out_specs, check_vma=False
    )
```

time: 187 us -> 148 us (0.79)
  the two profiles are of different devices: /device:TPU:0 before, /device:TPU:39 now
where the time goes in v3:
time: 148 us
  Pallas kernels  144 us (97%)
  local copies, waits for them, and re-layouts  2.53 us (2%)
    pallas_call x1, Pallas kernels, per_device(): pl.pallas_call(fused, out_shape=(jax.ShapeDtypeStruct((OWN, 2 * HALF), BF...  136 us
    pallas_call x1, Pallas kernels, per_device(): pl.pallas_call(finish, out_shape=(jax.ShapeDtypeStruct((OWN, D), BF16), g...  8.44 us

profile of v3, /device:TPU:39, one launch (start us, length us, event | category | flops | bytes accessed | tf_op | source)
XLA Modules:
  0.0 147.8 jit_solution(17799064567688331786)
XLA Ops:
  0.6 0.8 copy.11
  1.5 0.8 copy.10
  2.3 0.8 copy.12
  3.2 0.6 fusion.2.tables
  3.8 135.5 %attention_sublayer.1 = (bf16[320,3328]{1,0:T(8,128)(2,1)}, bf16[8,64,4992]{2,1,0:T(8,128)(2,1)}, bf16[2,208,896]{2,1,0:T(8,128)(2,1)}) custom-call(s32[3,8,8]{2,1,0:T(8,128)} %fusion.2.tables, bf16[200,1664]{1,0:T(8,128)(2,1)} %shard_hbm.1, bf16[8,64,4992]{2,1,0:T(8,128)(2,1)} %bitcast.12, bf16[320,3200]{1,0:T(8,128)(2,1)} %bitcast.14, f32[3200]{0:T(1024)} %scale.1), custom_call_target="tpu_custom_call" | custom-call | flops 12999999488 | bytes 20000000 | tf_op jit(solution)/shard_map/attention_sublayer/pallas_call | solution.py:627
  139.4 8.4 %finish.1 = (bf16[320,3200]{1,0:T(8,128)(2,1)}, bf16[8,64,4992]{2,1,0:T(8,128)(2,1)}, f32[200,1664]{1,0:T(8,128)}) custom-call(bf16[320,3328]{1,0:T(8,128)(2,1)} %get-tuple-element.9.branch_hbm, bf16[8,64,4992]{2,1,0:T(8,128)(2,1)} %get-tuple-element.10.grads_hbm, bf16[2,208,896]{2,1,0:T(8,128)(2,1)} %get-tuple-element.11.sums_hbm), custom_call_target="tpu_custom_call" | custom-call | tf_op jit(solution)/shard_map/finish/pallas_call | solution.py:693

commit v4 on v3

--- a/solution.py
+++ b/solution.py
@@ -19,7 +19,9 @@
 HALF = 8 * PADDED
 BLOCK = 896
 SECOND = WIDTH - BLOCK
+PARTS = ((0, BLOCK), (BLOCK, WIDTH))
 CUT = 96
+PIECE, STRIDE = 64, 48
 MASKED = -1e30
 TURNS = 0o06725341
 MESH = pl.DeviceIdType.MESH
@@ -54,15 +56,19 @@
 
 
 def unit_columns(unit):
-    return slice(2 * unit * HEAD, min(2 * unit + 2, HEADS) * HEAD)
-
-
-def by_columns(body):
-    @pl.loop(0, WIDTH // 256)
+    first = 2 * unit - (unit > 3)
+    return slice(first * HEAD, (first + 2 - (unit == 3)) * HEAD)
+
+
+def by_columns(body, first=0, last=WIDTH):
+    whole = (last - first) // 256
+
+    @pl.loop(0, whole)
     def _(n):
-        body(pl.multiple_of(n * 256, 128), 256)
-
-    body(WIDTH - WIDTH % 256, WIDTH % 256)
+        body(pl.multiple_of(first + n * 256, 128), 256)
+
+    if (last - first) % 256:
+        body(first + whole * 256, (last - first) % 256)
 
 
 def spread_tile(tile):
@@ -94,8 +100,8 @@
     branch_hbm, qkv_grad_hbm, final_hbm,
     meta, wv, wp, wh, qkv, sc, scale_parts, scale_pad, sp, sx, att_send, att_recv, aa, soft_keep,
     gh, relay, direct, total, relay2, direct2, summed, ysum, mixed, final,
-    ga_own, ga_send, ga_recv, back_send, back_recv, bx,
-    in_sem, w0s, w0r, w1s, w1r, a2s, a2r, cs, cr, g1s, g1r, g2s, g2r, ys, yr, fs, fr, b2s, b2r, out_sem,
+    ga_own, ga_send, ga_recv, back_send, back_first, back_second, bx, bp,
+    in_sem, w0s, w0r, w1s, w1r, w3s, w3r, a2s, a2r, cs, cr, g1s, g1r, g2s, g2r, ys, yr, fs, fr, b2s, b2r, out_sem,
 ):
     d = lax.axis_index("dp")
     f = lax.axis_index("fsdp")
@@ -124,13 +130,10 @@
     load_g.start()
 
     barrier = pltpu.get_barrier_semaphore()
-    peers = []
-    for step in range(1, 8):
-        other = (d + step) % 8
-        peers += [(other, f), (other, f + 1 - 2 * c)]
-    peers += [partner, at(x, y, z + 1, c), at(x, y, z - 1, c)]
-    for sign in (1, -1):
-        peers += [at(x, y + sign, z, 0), at(x, y + sign, z, 1)]
+    peers = [at(x, y, z + 1, c), at(x, y, z - 1, c), partner]
+    for place in range(1, 16):
+        for core in range(2):
+            peers.append(at(x + place % 4, y + place // 4, z, core))
     for peer in peers:
         pl.semaphore_signal(barrier, inc=1, device_id=peer, device_id_type=MESH)
     owner_of = [(d + 8 - tables[0, 0, k]) % 8 for k in range(IMGS)]
@@ -225,8 +228,12 @@
         remote(w_rows(z, 1), w_rows(z, 1), w1s.at[2], w1r.at[2], up),
         remote(w_rows(z, 0), w_rows(z, 0), w1s.at[3], w1r.at[3], down),
     ]
-    for copy in w1:
-        copy.start()
+
+    @pl.when(c == yl)
+    def _():
+        for copy in w1:
+            copy.start()
+
     w2 = [
         remote(w_rows(z - 1, 0), w_rows(z - 1, 0), w1s.at[4], w1r.at[4], up),
         remote(w_rows(z + 1, 1), w_rows(z + 1, 1), w1s.at[5], w1r.at[5], down),
@@ -270,10 +277,28 @@
         parts = mm(scale_parts[:, pl.ds(pl.multiple_of(start, 128), 256)], pick)
         scale_pad[:, there] = jnp.sum(parts, axis=0, keepdims=True)
 
-    w1[0].wait_recv()
-    w2[0].start()
-    w1[1].wait_recv()
-    w2[1].start()
+    def w_on(step, k):
+        pz = z + (1, -1, 2)[step]
+        sem = 2 * step + k
+        return remote(
+            w_rows(pz, k), w_rows(pz, k), w3s.at[sem], w3r.at[sem], at(x, y + 1 - 2 * k, z, c)
+        )
+
+    @pl.when(c == yl)
+    def _():
+        w1[0].wait_recv()
+        w2[0].start()
+        w_on(1, 0).start()
+        w1[1].wait_recv()
+        w2[1].start()
+        w_on(0, 1).start()
+        w1[2].wait_recv()
+        w_on(1, 1).start()
+        w1[3].wait_recv()
+        w_on(0, 0).start()
+        for k in range(2):
+            w2[k].wait_recv()
+            w_on(2, k).start()
 
     for i in range(7):
         source = partner_at(i, -1)
@@ -301,12 +326,14 @@
 
     def block(first, second):
         first, second = (first + 4) % 4, (second + 4) % 4
-        return first % 2, pl.ds(pl.multiple_of((second * 2 + first // 2) * PADDED, 16), PADDED)
-
-    p1 = y * (1 - c) + x * c
-    p2 = z
-    right1, left1 = at(x + c, y + 1 - c, z, c), at(x - c, y - 1 + c, z, c)
-    right2, left2 = up, down
+        pz = first * (1 - c) + second * c
+        kh = second * (1 - c) + first * c
+        return kh % 2, pl.ds(pl.multiple_of((pz * 2 + kh // 2) * PADDED, 16), PADDED)
+
+    p1 = z * (1 - c) + x * c
+    p2 = y * (1 - c) + z * c
+    right1, left1 = at(x + c, y, z + 1 - c, c), at(x - c, y, z - 1 + c, c)
+    right2, left2 = at(x, y + 1 - c, z + c, c), at(x, y - 1 + c, z - c, c)
 
     def g1(first, j, dst, sem, dev):
         h, rows = block(first, j)
@@ -325,11 +352,11 @@
             rows = pl.ds(pl.multiple_of(t * 128, 128), 128)
             gh[h, rows, :] = mm(sp[:, rows], aa[:, cols], TN).astype(BF16)
 
-    weight_columns(p1 % 2)
-    for copy in (s1[0], s1[2], s1[1], s1[3]):
-        copy.start()
-    weight_columns(1 - p1 % 2)
-    for copy in (s1[4], s1[6], s1[5], s1[7]):
+    weight_columns(0)
+    weight_columns(1)
+    first_sends = [s1[n] for n in (0, 2, 1, 3, 4, 6, 5, 7)]
+
+    for copy in first_sends:
         copy.start()
     r1 = [g1(p1 + 1, j, direct.at[0, j], 4 + j, right1) for j in (0, 1)]
     r1 += [g1(p1 - 1, j, direct.at[1, j], 8 + j, left1) for j in (2, 3)]
@@ -339,35 +366,25 @@
         def _(r):
             body(pl.multiple_of(r * 16, 16))
 
-    for n, j in enumerate((0, 2, 1, 3)):
-        side, place = (0, p1 + 1) if j < 2 else (1, p1 - 1)
-        s1[j].wait_recv()
-        h, rows = block(place, j)
-        base = rows.start
-
-        def add_relay(r, h=h, base=base, side=side, j=j):
-            here = pl.ds(pl.multiple_of(base + r, 16), 16)
-            gh[h, here, :] = (
-                gh[h, here, :].astype(F32) + relay[side, j % 2, pl.ds(r, 16), :].astype(F32)
-            ).astype(BF16)
-
-        add_rows(PADDED, add_relay)
-        r1[j].start()
-
-    w1[2].wait_recv()
-    w1[3].wait_recv()
-    w2[0].wait_recv()
-    w2[1].wait_recv()
+    @pl.when(c != yl)
+    def _():
+        for step in range(3):
+            for k in range(2):
+                w_on(step, k).wait_recv()
 
     def grad_columns(start, size):
         cols = pl.ds(start, size)
         ga_send[:, cols] = mm(sp[other_rows, :], wh[:, cols])
         ga_own[:, cols] = mm(sp[own_rows, :], wh[:, cols])
 
-    by_columns(grad_columns)
-    send_ga = remote(ga_send, ga_recv, cs.at[2], cr.at[2], partner)
-    send_ga.start()
-    send_ga.wait_recv()
+    send_ga = []
+    for n, (first, last) in enumerate(PARTS):
+        by_columns(grad_columns, first, last)
+        cols = pl.ds(first, last - first)
+        send_ga.append(
+            remote(ga_send.at[:, cols], ga_recv.at[:, cols], cs.at[2 + n], cr.at[2 + n], partner)
+        )
+        send_ga[n].start()
     unpack = []
     for n in range(8):
         inside = lax.broadcasted_iota(jnp.int32, (MAXP, OWN), 0)
@@ -381,15 +398,38 @@
         grad = (ga_own[:, cols] + ga_recv[:, cols]).astype(BF16)
         back_send[:, :, cols] = mm(unpack, grad).astype(BF16).reshape(IMGS, MAXP, size)
 
-    by_columns(unpack_columns)
-
-    def back_copy(i):
+    back_parts = (back_first, back_second)
+
+    def back_copy(i, n):
         loader = partner_at(i)
-        return remote(back_send.at[loader], back_recv.at[d], b2s.at[i], b2r.at[i], (loader, f))
-
-    for i in range(7):
-        back_copy(i).start()
-    back_recv[d] = back_send[d]
+        cols = pl.ds(PARTS[n][0], PARTS[n][1] - PARTS[n][0])
+        return remote(
+            back_send.at[loader, :, cols], back_parts[n].at[d],
+            b2s.at[7 * n + i], b2r.at[7 * n + i], (loader, f),
+        )
+
+    for n, j in enumerate((0, 2, 1, 3)):
+        side, place = (0, p1 + 1) if j < 2 else (1, p1 - 1)
+        s1[j].wait_recv()
+        h, rows = block(place, j)
+        base = rows.start
+
+        def add_relay(r, h=h, base=base, side=side, j=j):
+            here = pl.ds(pl.multiple_of(base + r, 16), 16)
+            gh[h, here, :] = (
+                gh[h, here, :].astype(F32) + relay[side, j % 2, pl.ds(r, 16), :].astype(F32)
+            ).astype(BF16)
+
+        add_rows(PADDED, add_relay)
+        r1[j].start()
+
+    for n in range(2):
+        send_ga[n].wait_recv()
+        by_columns(unpack_columns, *PARTS[n])
+        for i in range(7):
+            back_copy(i, n).start()
+    for n in range(2):
+        back_parts[n][d] = back_send[d, :, PARTS[n][0] : PARTS[n][1]]
 
     for j in range(4):
         (s1[4 + j - 2] if j >= 2 else r1[j]).wait_recv()
@@ -430,12 +470,12 @@
         bx[:, cols] = (scale_pad[:, cols] * mm(aa[...], wh[cols, :], NT)).astype(BF16)
 
     by_columns(project_rows)
-    my_half = branch_hbm.at[:, pl.ds(pl.multiple_of(c * HALF, 128), HALF)]
-    other_half = branch_hbm.at[:, pl.ds(pl.multiple_of((1 - c) * HALF, 128), HALF)]
-    send_bx = remote(bx.at[other_rows, :], my_half, cs.at[3], cr.at[3], partner)
+    my_half = bp.at[:, pl.ds(pl.multiple_of(c * HALF, 128), HALF)]
+    other_half = bp.at[:, pl.ds(pl.multiple_of((1 - c) * HALF, 128), HALF)]
+    send_bx = remote(bx.at[other_rows, :], my_half, cs.at[4], cr.at[4], partner)
     send_bx.start()
-    store_branch = pltpu.make_async_copy(bx.at[own_rows, :], my_half, out_sem.at[8])
-    store_branch.start()
+    keep_bx = pltpu.make_async_copy(bx.at[own_rows, :], my_half, out_sem.at[10])
+    keep_bx.start()
 
     for side in range(2):
         s2[side].wait_recv()
@@ -464,21 +504,77 @@
 
     add_rows(PADDED, add_second)
 
+    p3 = x * (1 - c) + y * c
+
+    def piece(place):
+        return pl.ds(pl.multiple_of((place + 4) % 4 * STRIDE, 16), PIECE)
+
     s3 = [
-        remote(summed, ysum.at[n], ys.at[n], yr.at[n], at(x + (1 - c) * m, y + c * m, z, c))
+        remote(
+            summed.at[piece(p3 + m), :], ysum.at[n], ys.at[n], yr.at[n],
+            at(x + (1 - c) * m, y + c * m, z, c),
+        )
         for n, m in enumerate((1, 3, 2))
     ]
     for copy in s3:
         copy.start()
 
-    def backward(slot):
+    keep_bx.wait()
+    remote(bx.at[other_rows, :], other_half, cs.at[4], cr.at[4], partner).wait_recv()
+
+    @pl.loop(0, D // 128, unroll=5)
+    def _(t):
+        start, pick = compact_tile(t)
+        window = bp[:, pl.ds(pl.multiple_of(start, 128), 384)]
+        sc[:, pl.ds(pl.multiple_of(t * 128, 128), 128)] = mm(window, pick).astype(BF16)
+
+    store_branch = pltpu.make_async_copy(sc, branch_hbm, out_sem.at[8])
+    store_branch.start()
+
+    for copy in s3:
+        copy.wait_recv()
+
+    @pl.loop(0, PIECE // 16)
+    def _(r):
+        here = pl.ds(pl.multiple_of(r * 16, 16), 16)
+        there = pl.ds(pl.multiple_of(p3 * STRIDE + r * 16, 16), 16)
+        mixed[here, :] = (
+            summed[there, :].astype(F32)
+            + ysum[0, here, :].astype(F32)
+            + ysum[1, here, :].astype(F32)
+            + ysum[2, here, :].astype(F32)
+        ).astype(BF16)
+
+    kept = y * (1 - c) + x * c
+    keeper = kept // 2
+    column = kept % 2
+    mine = (c == yl) & (keeper == c)
+
+    def for_spread(act):
+        for n in (1, 3, 2, 0):
+            for m in range(2):
+                copy = remote(
+                    mixed, final.at[column, p3], fs.at[2 * n + m], fr.at[column * 4 + p3],
+                    at(x + n, c + 2 * m, z, keeper),
+                )
+                if n:
+                    act(copy)
+                else:
+                    @pl.when(jnp.logical_not((y == c + 2 * m) & (keeper == c)))
+                    def _():
+                        act(copy)
+
+    for_spread(lambda copy: copy.start())
+
+    def backward(slot, groups):
         owner = meta[2, slot]
-        for units in ((0, 1, 2), (3, 4), (5, 6)):
+        for units in groups:
             stages = []
             for u in units:
                 cols = unit_columns(u)
                 v = qkv[slot, :, 2 * WIDTH + cols.start : 2 * WIDTH + cols.stop]
-                go = stacked(back_recv[owner, :, cols])
+                skip, got = (0, back_first) if u < 4 else (BLOCK, back_second)
+                go = stacked(got[owner, :, cols.start - skip : cols.stop - skip])
                 soft = soft_keep[owner, u, :, : go.shape[0]]
                 stages.append((u, go, soft, mm(v, go, NT)))
             for u, go, soft, grad_soft in stages:
@@ -498,80 +594,62 @@
     def store_slot(slot):
         return pltpu.make_async_copy(qkv.at[slot], qkv_grad_hbm.at[slot], out_sem.at[slot])
 
-    for copy in s3:
-        copy.wait_recv()
-
-    def add_third(r):
-        here = pl.ds(r, 16)
-        mixed[here, :] = (
-            summed[here, :].astype(F32)
-            + ysum[0, here, :].astype(F32)
-            + ysum[1, here, :].astype(F32)
-            + ysum[2, here, :].astype(F32)
-        ).astype(BF16)
-
-    add_rows(PADDED, add_third)
-    keeper = p1 // 2
-    column = p1 % 2
-    mine = (c == yl) & (keeper == c)
-
-    def f_copy(n, dev):
-        return remote(mixed, final.at[column], fs.at[n], fr.at[column], dev)
-
-    f_y = [f_copy(n, at(x, 2 * n, z, keeper)) for n in range(2)]
-    f_x = [f_copy(n, at(x + n, y, z, keeper)) for n in range(4)]
-
-    def for_spread(act):
-        for n in range(2):
-            @pl.when((c == 0) & jnp.logical_not(mine & (y == 2 * n)))
-            def _():
-                act(f_y[n])
-
-        @pl.when((c == 1) & (yl == 1))
-        def _():
-            for n in (1, 3, 2):
-                act(f_x[n])
-
-            @pl.when(jnp.logical_not(mine))
-            def _():
-                act(f_x[0])
-
-    for_spread(lambda copy: copy.start())
-
-    for i in range(7):
-        source = partner_at(i, -1)
-        remote(back_send.at[source], back_recv.at[source], b2s.at[i], b2r.at[i], partner).wait_recv()
+    def wait_back(n):
+        for i in range(7):
+            source = partner_at(i, -1)
+            cols = pl.ds(PARTS[n][0], PARTS[n][1] - PARTS[n][0])
+            remote(
+                back_send.at[source, :, cols], back_parts[n].at[source],
+                b2s.at[7 * n + i], b2r.at[7 * n + i], partner,
+            ).wait_recv()
+
+    wait_back(0)
 
     @pl.loop(0, IMGS)
     def _(slot):
-        backward(slot)
+        backward(slot, ((0, 1), (2, 3)))
+
+    wait_back(1)
+
+    @pl.loop(0, IMGS)
+    def _(slot):
+        backward(slot, ((4, 5, 6),))
         store_slot(slot).start()
 
     for n in range(2):
-        @pl.when(mine & (column == n))
-        def _():
-            final[n] = mixed[...]
-
-        @pl.when(jnp.logical_not(mine & (column == n)))
-        def _():
-            remote(mixed, final.at[n], fs.at[0], fr.at[n], partner).wait_recv()
+        for q in range(4):
+            own = mine & (column == n) & (p3 == q)
+
+            @pl.when(own)
+            def _():
+                final[n, q] = mixed[...]
+
+            @pl.when(jnp.logical_not(own))
+            def _():
+                remote(mixed, final.at[n, q], fs.at[0], fr.at[n * 4 + q], partner).wait_recv()
 
     store_w = pltpu.make_async_copy(final, final_hbm, out_sem.at[9])
     store_w.start()
-    send_bx_recv = remote(bx.at[other_rows, :], other_half, cs.at[3], cr.at[3], partner)
-    send_bx_recv.wait_recv()
-
     w_y.wait_send()
 
     @pl.when(c != yl)
     def _():
         w_c.wait_send()
 
+    @pl.when(c == yl)
+    def _():
+        for copy in (*w1, *w2):
+            copy.wait_send()
+        for step in range(3):
+            for k in range(2):
+                w_on(step, k).wait_send()
+
     for_spread(lambda copy: copy.wait_send())
     for i in range(7):
         att_copy(i).wait_send()
-        back_copy(i).wait_send()
-    for copy in (*w1, *w2, send_sx, send_aa, send_ga, send_bx, *s1, *r1, *s2, *r2, *s3):
+        back_copy(i, 0).wait_send()
+        back_copy(i, 1).wait_send()
+    for copy in (send_sx, send_aa, *send_ga, send_bx, *s1, *r1, *s2, *r2, *s3):
         copy.wait_send()
     for slot in range(IMGS):
         store_slot(slot).wait()
@@ -581,33 +659,29 @@
 
 def finish(
     branch_hbm, grads_hbm, sums_hbm, branch_out, grads_out, weight_out,
-    padded, grads, sums, branch, weight, in_sem, out_sem,
+    branch, grads, sums, weight, in_sem, out_sem,
 ):
-    load_branch = pltpu.make_async_copy(branch_hbm, padded, in_sem.at[8])
+    load_branch = pltpu.make_async_copy(branch_hbm, branch, in_sem.at[8])
     load_sums = pltpu.make_async_copy(sums_hbm, sums, in_sem.at[9])
     loads = [pltpu.make_async_copy(grads_hbm.at[k], grads.at[k], in_sem.at[k]) for k in range(IMGS)]
     stores = [pltpu.make_async_copy(grads.at[k], grads_out.at[k], out_sem.at[k]) for k in range(IMGS)]
     store_branch = pltpu.make_async_copy(branch, branch_out, out_sem.at[8])
     store_weight = pltpu.make_async_copy(weight, weight_out, out_sem.at[9])
-    load_branch.start()
     load_sums.start()
     for load in loads:
         load.start()
+    load_branch.start()
     load_sums.wait()
-    weight[:, :BLOCK] = sums[0].astype(F32)[:SHARD]
-    weight[:, SECOND:] = sums[1].astype(F32)[:SHARD]
+    for q in range(4):
+        size = STRIDE if q < 3 else SHARD - 3 * STRIDE
+        here = slice(q * STRIDE, q * STRIDE + size)
+        weight[here, :BLOCK] = sums[0, q].astype(F32)[:size]
+        weight[here, SECOND:] = sums[1, q].astype(F32)[:size]
     store_weight.start()
-    load_branch.wait()
     for k in range(IMGS):
         loads[k].wait()
         stores[k].start()
-
-    @pl.loop(0, D // 128, unroll=5)
-    def _(t):
-        start, pick = compact_tile(t)
-        window = padded[:, pl.ds(pl.multiple_of(start, 128), 384)]
-        branch[:, pl.ds(pl.multiple_of(t * 128, 128), 128)] = mm(window, pick).astype(BF16)
-
+    load_branch.wait()
     store_branch.start()
     for store in (store_weight, *stores, store_branch):
         store.wait()
@@ -616,20 +690,22 @@
 def per_device(
     qkv_rows, proj_weight, layer_scale, out_grad, patch_counts, loader_plan, row_offsets
 ):
-    tables = jnp.stack([loader_plan, patch_counts, row_offsets])
-    tables = lax.dynamic_index_in_dim(tables, lax.axis_index("fsdp"), 2, keepdims=False)
+    tables = [jnp.swapaxes(table, 1, 2) for table in (loader_plan, patch_counts, row_offsets)]
+    tables = lax.dynamic_index_in_dim(
+        jnp.stack(tables), lax.axis_index("fsdp"), 3, keepdims=False
+    )
     vmem = pl.BlockSpec(memory_space=pltpu.VMEM)
     smem = pl.BlockSpec(memory_space=pltpu.SMEM)
     hbm = pl.BlockSpec(memory_space=pl.ANY)
     dma = pltpu.SemaphoreType.DMA
     rows = (PADDED, BLOCK)
     grads_shape = jax.ShapeDtypeStruct((IMGS, MAXP, 3 * WIDTH), BF16)
-    padded_branch, grads, sums = pl.pallas_call(
+    branch, grads, sums = pl.pallas_call(
         fused,
         out_shape=(
-            jax.ShapeDtypeStruct((OWN, 2 * HALF), BF16),
+            jax.ShapeDtypeStruct((OWN, D), BF16),
             grads_shape,
-            jax.ShapeDtypeStruct((2, *rows), BF16),
+            jax.ShapeDtypeStruct((2, 4, PIECE, BLOCK), BF16),
         ),
         in_specs=[smem, hbm, hbm, hbm, vmem],
         out_specs=(hbm, hbm, hbm),
@@ -655,26 +731,29 @@
             pltpu.VMEM(rows, BF16),
             pltpu.VMEM((2, *rows), BF16),
             pltpu.VMEM(rows, BF16),
-            pltpu.VMEM((3, *rows), BF16),
-            pltpu.VMEM(rows, BF16),
-            pltpu.VMEM((2, *rows), BF16),
+            pltpu.VMEM((3, PIECE, BLOCK), BF16),
+            pltpu.VMEM((PIECE, BLOCK), BF16),
+            pltpu.VMEM((2, 4, PIECE, BLOCK), BF16),
             pltpu.VMEM((OWN, WIDTH), F32),
             pltpu.VMEM((OWN, WIDTH), F32),
             pltpu.VMEM((OWN, WIDTH), F32),
             pltpu.VMEM((IMGS, MAXP, WIDTH), BF16),
-            pltpu.VMEM((IMGS, MAXP, WIDTH), BF16),
+            pltpu.VMEM((IMGS, MAXP, BLOCK), BF16),
+            pltpu.VMEM((IMGS, MAXP, WIDTH - BLOCK), BF16),
             pltpu.VMEM((2 * OWN, HALF), BF16),
+            pltpu.VMEM((OWN, 2 * HALF), BF16),
             dma((3,)),
             dma((2,)), dma((2,)),
             dma((6,)), dma((6,)),
+            dma((6,)), dma((6,)),
             dma((7,)), dma((7,)),
-            dma((4,)), dma((4,)),
+            dma((5,)), dma((5,)),
             dma((12,)), dma((12,)),
             dma((6,)), dma((6,)),
             dma((3,)), dma((3,)),
-            dma((4,)), dma((2,)),
-            dma((7,)), dma((7,)),
-            dma((10,)),
+            dma((8,)), dma((8,)),
+            dma((14,)), dma((14,)),
+            dma((11,)),
         ],
         compiler_params=pltpu.CompilerParams(
             collective_id=0, has_side_effects=True, vmem_limit_bytes=62 << 20
@@ -690,7 +769,7 @@
         out_grad[0, 0],
         layer_scale,
     )
-    branch, grads, weight_grad = pl.pallas_call(
+    branch_rows, grads, weight_grad = pl.pallas_call(
         finish,
         out_shape=(
             jax.ShapeDtypeStruct((OWN, D), BF16),
@@ -700,18 +779,17 @@
         in_specs=[hbm, hbm, hbm],
         out_specs=(hbm, hbm, hbm),
         scratch_shapes=[
-            pltpu.VMEM((OWN, 2 * HALF), BF16),
+            pltpu.VMEM((OWN, D), BF16),
             pltpu.VMEM((IMGS, MAXP, 3 * WIDTH), BF16),
-            pltpu.VMEM((2, *rows), BF16),
-            pltpu.VMEM((OWN, D), BF16),
+            pltpu.VMEM((2, 4, PIECE, BLOCK), BF16),
             pltpu.VMEM((SHARD, WIDTH), F32),
             dma((10,)),
             dma((10,)),
         ],
         compiler_params=pltpu.CompilerParams(vmem_limit_bytes=60 << 20),
         name="finish",
-    )(padded_branch, grads, sums)
-    return (branch[None, None], grads[None, None], weight_grad)
+    )(branch, grads, sums)
+    return (branch_rows[None, None], grads[None, None], weight_grad)
 
 
 def solution(mesh):

time: 148 us -> 134 us (0.905)
  the two profiles are of different devices: /device:TPU:39 before, /device:TPU:0 now
where the time goes in v4:
time: 134 us; the launch traced here: 132 us
  Pallas kernels  128 us (96%)
  local copies, waits for them, and re-layouts  2.53 us (2%)
    pallas_call x1, Pallas kernels, per_device(): pl.pallas_call(fused, out_shape=(jax.ShapeDtypeStruct((OWN, D), BF16), gr...  121 us
    pallas_call x1, Pallas kernels, per_device(): pl.pallas_call(finish, out_shape=(jax.ShapeDtypeStruct((OWN, D), BF16), g...  7.15 us

profile of v4, /device:TPU:0, one launch (start us, length us, event | category | flops | bytes accessed | tf_op | source)
XLA Modules:
  0.0 131.9 jit_solution(13599629586721952035)
XLA Ops:
  0.6 0.8 copy.11
  1.5 0.8 copy.10
  2.3 0.8 copy.12
  3.2 0.6 fusion.2.tables
  3.8 120.9 %attention_sublayer.1 = (bf16[320,3200]{1,0:T(8,128)(2,1)}, bf16[8,64,4992]{2,1,0:T(8,128)(2,1)}, bf16[2,4,64,896]{3,2,1,0:T(8,128)(2,1)}) custom-call(s32[3,8,8]{2,1,0:T(8,128)} %fusion.2.tables, bf16[200,1664]{1,0:T(8,128)(2,1)} %shard_hbm.1, bf16[8,64,4992]{2,1,0:T(8,128)(2,1)} %bitcast.18, bf16[320,3200]{1,0:T(8,128)(2,1)} %bitcast.20, f32[3200]{0:T(1024)} %scale.1), custom_call_target="tpu_custom_call" | custom-call | flops 12999999488 | bytes 20000000 | tf_op jit(solution)/shard_map/attention_sublayer/pallas_call | solution.py:703
  124.7 7.1 %finish.1 = (bf16[320,3200]{1,0:T(8,128)(2,1)}, bf16[8,64,4992]{2,1,0:T(8,128)(2,1)}, f32[200,1664]{1,0:T(8,128)}) custom-call(bf16[320,3200]{1,0:T(8,128)(2,1)} %get-tuple-element.9.branch_hbm, bf16[8,64,4992]{2,1,0:T(8,128)(2,1)} %get-tuple-element.10.grads_hbm, bf16[2,4,64,896]{3,2,1,0:T(8,128)(2,1)} %get-tuple-element.11.sums_hbm), custom_call_target="tpu_custom_call" | custom-call | tf_op jit(solution)/shard_map/finish/pallas_call | solution.py:772

commit v5 on v4

--- a/solution.py
+++ b/solution.py
@@ -96,7 +96,7 @@
 
 
 def fused(
-    tables, shard_hbm, qkv_hbm, grad_hbm, scale,
+    plan, counts, offsets, shard_hbm, qkv_hbm, grad_hbm, scale,
     branch_hbm, qkv_grad_hbm, final_hbm,
     meta, wv, wp, wh, qkv, sc, scale_parts, scale_pad, sp, sx, att_send, att_recv, aa, soft_keep,
     gh, relay, direct, total, relay2, direct2, summed, ysum, mixed, final,
@@ -136,7 +136,7 @@
             peers.append(at(x + place % 4, y + place // 4, z, core))
     for peer in peers:
         pl.semaphore_signal(barrier, inc=1, device_id=peer, device_id_type=MESH)
-    owner_of = [(d + 8 - tables[0, 0, k]) % 8 for k in range(IMGS)]
+    owner_of = [(d + 8 - plan[0, k, f]) % 8 for k in range(IMGS)]
     for k in range(IMGS):
         meta[2, k] = owner_of[k]
     image_offset, image_count = [], []
@@ -144,11 +144,11 @@
         slot, image = 0, 0
         for k in range(1, IMGS):
             slot = jnp.where(owner_of[k] == e, k, slot)
-            image = jnp.where(tables[0, d, k] == e, k, image)
+            image = jnp.where(plan[d, k, f] == e, k, image)
         meta[0, e] = slot
-        meta[1, e] = tables[1, e, slot]
-        image_offset.append(tables[2, d, image])
-        image_count.append(tables[1, d, image])
+        meta[1, e] = counts[e, slot, f]
+        image_offset.append(offsets[d, image, f])
+        image_count.append(counts[d, image, f])
     load_w.wait()
     wp[0:192, :] = wv[0:192, :]
     wp[192:208, :] = jnp.concatenate(
@@ -431,6 +431,18 @@
     for n in range(2):
         back_parts[n][d] = back_send[d, :, PARTS[n][0] : PARTS[n][1]]
 
+    def project_rows(start, size):
+        cols = pl.ds(start, size)
+        bx[:, cols] = (scale_pad[:, cols] * mm(aa[...], wh[cols, :], NT)).astype(BF16)
+
+    by_columns(project_rows)
+    my_half = bp.at[:, pl.ds(pl.multiple_of(c * HALF, 128), HALF)]
+    other_half = bp.at[:, pl.ds(pl.multiple_of((1 - c) * HALF, 128), HALF)]
+    send_bx = remote(bx.at[other_rows, :], my_half, cs.at[4], cr.at[4], partner)
+    send_bx.start()
+    keep_bx = pltpu.make_async_copy(bx.at[own_rows, :], my_half, out_sem.at[10])
+    keep_bx.start()
+
     for j in range(4):
         (s1[4 + j - 2] if j >= 2 else r1[j]).wait_recv()
         (s1[6 + j] if j < 2 else r1[j]).wait_recv()
@@ -464,18 +476,6 @@
     ]
     for copy in s2:
         copy.start()
-
-    def project_rows(start, size):
-        cols = pl.ds(start, size)
-        bx[:, cols] = (scale_pad[:, cols] * mm(aa[...], wh[cols, :], NT)).astype(BF16)
-
-    by_columns(project_rows)
-    my_half = bp.at[:, pl.ds(pl.multiple_of(c * HALF, 128), HALF)]
-    other_half = bp.at[:, pl.ds(pl.multiple_of((1 - c) * HALF, 128), HALF)]
-    send_bx = remote(bx.at[other_rows, :], my_half, cs.at[4], cr.at[4], partner)
-    send_bx.start()
-    keep_bx = pltpu.make_async_copy(bx.at[own_rows, :], my_half, out_sem.at[10])
-    keep_bx.start()
 
     for side in range(2):
         s2[side].wait_recv()
@@ -691,9 +691,6 @@
     qkv_rows, proj_weight, layer_scale, out_grad, patch_counts, loader_plan, row_offsets
 ):
     tables = [jnp.swapaxes(table, 1, 2) for table in (loader_plan, patch_counts, row_offsets)]
-    tables = lax.dynamic_index_in_dim(
-        jnp.stack(tables), lax.axis_index("fsdp"), 3, keepdims=False
-    )
     vmem = pl.BlockSpec(memory_space=pltpu.VMEM)
     smem = pl.BlockSpec(memory_space=pltpu.SMEM)
     hbm = pl.BlockSpec(memory_space=pl.ANY)
@@ -707,7 +704,7 @@
             grads_shape,
             jax.ShapeDtypeStruct((2, 4, PIECE, BLOCK), BF16),
         ),
-        in_specs=[smem, hbm, hbm, hbm, vmem],
+        in_specs=[smem, smem, smem, hbm, hbm, hbm, vmem],
         out_specs=(hbm, hbm, hbm),
         scratch_shapes=[
             pltpu.SMEM((3, 8), jnp.int32),
@@ -763,7 +760,7 @@
         ),
         name="attention_sublayer",
     )(
-        tables,
+        *tables,
         proj_weight,
         qkv_rows[0, 0],
         out_grad[0, 0],

time: 134 us -> 132 us (0.985)
  local copies, waits for them, and re-layouts: 2.53 us -> 0 us
    unnamed x3 -> x0, local copies, waits for them, and re-layouts: 2.53 us -> none
where the time goes in v5:
time: 132 us; the launch traced here: 129 us
  Pallas kernels  129 us (98%)
    pallas_call x1, Pallas kernels, per_device(): pl.pallas_call(fused, out_shape=(jax.ShapeDtypeStruct((OWN, D), BF16), gr...  122 us
    pallas_call x1, Pallas kernels, per_device(): pl.pallas_call(finish, out_shape=(jax.ShapeDtypeStruct((OWN, D), BF16), g...  7.15 us

profile of v5, /device:TPU:0, one launch (start us, length us, event | category | flops | bytes accessed | tf_op | source)
XLA Modules:
  0.0 129.5 jit_solution(11981806952062473420)
XLA Ops:
  0.6 121.7 %attention_sublayer.1 = (bf16[320,3200]{1,0:T(8,128)(2,1)}, bf16[8,64,4992]{2,1,0:T(8,128)(2,1)}, bf16[2,4,64,896]{3,2,1,0:T(8,128)(2,1)}) custom-call(s32[8,8,16]{2,1,0:T(8,128)} %bitcast.11, s32[8,8,16]{2,1,0:T(8,128)} %bitcast.12, s32[8,8,16]{2,1,0:T(8,128)} %bitcast.13, bf16[200,1664]{1,0:T(8,128)(2,1)} %shard_hbm.1, bf16[8,64,4992]{2,1,0:T(8,128)(2,1)} %bitcast.7, ...), custom_call_target="tpu_custom_call" | custom-call | flops 12999999488 | bytes 20000000 | tf_op jit(solution)/shard_map/attention_sublayer/pallas_call | solution.py:700
  122.3 7.1 %finish.1 = (bf16[320,3200]{1,0:T(8,128)(2,1)}, bf16[8,64,4992]{2,1,0:T(8,128)(2,1)}, f32[200,1664]{1,0:T(8,128)}) custom-call(bf16[320,3200]{1,0:T(8,128)(2,1)} %get-tuple-element.9.branch_hbm, bf16[8,64,4992]{2,1,0:T(8,128)(2,1)} %get-tuple-element.10.grads_hbm, bf16[2,4,64,896]{3,2,1,0:T(8,128)(2,1)} %get-tuple-element.11.sums_hbm), custom_call_target="tpu_custom_call" | custom-call | tf_op jit(solution)/shard_map/finish/pallas_call | solution.py:769
